TPU v7x, 128 devices: a whole 4x4x4 slice. The times are simulated.
128 devices in a mesh: ctx: 16 (over z, y), head: 8 (over x, core).
Axes of the slice: x: 4, y: 4, z: 4, core: 2. Of those that a mesh axis runs over, the one named last changes fastest.
Arguments:
- g_out: bfloat16 [8192, 8192], P('ctx', 'head'), may hold values from -6 to 6
- w_out: bfloat16 [8192, 8192], P('ctx', 'head'), may hold values from -0.0625 to 0.0625
- x_act: bfloat16 [8192, 8192], P('ctx', 'head'), may hold values from -6 to 6
- b_proj: bfloat16 [8192, 128], P('ctx'), may hold values from -0.5 to 0.5
- c_proj: bfloat16 [8192, 128], P('ctx'), may hold values from -0.0625 to 0.0625
- log_decay: float32 [128, 8192], P('head', 'ctx'), may hold values from -2 to 0
- kept_heads: int32 [64], replicated, may hold values from 0 to 127, as said below
Outputs:
- input_grad: bfloat16 [8192, 8192], P('ctx', 'head')
- b_grad: float32 [8192, 128], P('ctx')
- c_grad: float32 [8192, 128], P('ctx')
- decay_grad: float32 [128, 8192], P('head', 'ctx')
- weight_grad: bfloat16 [8192, 8192], P('ctx', 'head')
Inputs may be any that keep to these rules, and one draw needn't show every extreme that they name: `kept_heads`: kept head indices are distinct and increasing; at most 12 of them fall in any group of 16 consecutive heads starting at a multiple of 16, and exactly 12 in one such group.
All inputs are finite; a program needn't handle non-finite values.
Results may differ from a plain program's by a relative error of at most 0.024.
Values may be sent and summed in bfloat16 or wider, within the bound.
A program may use at most 128 MiB of HBM per device.

v0:
```python
import math

import jax
import jax.numpy as jnp
from jax import lax
from jax.sharding import PartitionSpec as P

P_SIZE = 64
N = 128
KEPT = 64
Q = 128


highest = lax.Precision.HIGHEST


def entering_2(array, axis, join, neutral, backward):
    count = lax.axis_size(axis)
    place = lax.axis_index(axis)
    ahead = count - 1 - place if backward else place
    gathered = jax.tree.map(
        lambda a, kind: lax.all_gather(a.astype(kind), axis), array, (jnp.bfloat16, jnp.bfloat16)
    )
    state = jax.tree.map(lambda a, e: jnp.zeros_like(a) + jnp.asarray(e, a.dtype), array, neutral)

    def one(step, state):
        source = count - 1 - step if backward else step
        return join(
            state,
            jax.tree.map(
                lambda a, own: lax.dynamic_index_in_dim(a, source, 0, False).astype(own.dtype),
                gathered,
                array,
            ),
        )

    return lax.fori_loop(0, ahead, one, state)


def state_terms(cumulative, span_total, inputs, b_mat):
    tail = jnp.exp(span_total[..., None] - cumulative)
    return jnp.einsum("scip,scin->scpn", inputs, tail[..., None] * b_mat[None], precision=highest)


def adjoint_terms(cumulative, out_grad, c_mat):
    return jnp.einsum(
        "sctp,sctn->scpn", out_grad, jnp.exp(cumulative)[..., None] * c_mat[None], precision=highest
    )


def fold_forward(span_total, parts):

    def advance(state, inputs_now):
        total_now, part_now = inputs_now
        return (jnp.exp(total_now)[:, None, None] * state + part_now, state)

    closing, entering = lax.scan(
        advance, jnp.zeros_like(parts[:, 0]), (jnp.transpose(span_total), jnp.moveaxis(parts, 1, 0))
    )
    return (closing, jnp.moveaxis(entering, 0, 1))


def fold_backward(span_total, parts):

    def advance(state, inputs_now):
        total_now, part_now = inputs_now
        return (jnp.exp(total_now)[:, None, None] * state + part_now, state)

    opening, ending = lax.scan(
        advance,
        jnp.zeros_like(parts[:, 0]),
        (jnp.transpose(span_total), jnp.moveaxis(parts, 1, 0)),
        reverse=True,
    )
    return (opening, jnp.moveaxis(ending, 0, 1))


def span_outputs(cumulative, span_total, inputs, b_mat, c_mat, out_grad, state_in, adjoint_end):
    length = cumulative.shape[-1]
    triangle = jnp.tril(jnp.ones((length, length), jnp.float32))
    allowed = triangle > 0.5
    differ = cumulative[..., :, None] - cumulative[..., None, :]
    weights_low = jnp.where(allowed, jnp.exp(jnp.where(allowed, differ, 0.0)), 0.0)
    cross_cb = jnp.einsum("ctn,cin->cti", c_mat, b_mat, precision=highest)
    cross_gx = jnp.einsum("sctp,scip->scti", out_grad, inputs, precision=highest)
    mixed_cb = weights_low * cross_cb[None]
    mixed_gx = weights_low * cross_gx
    head_w = jnp.exp(cumulative)
    tail = jnp.exp(span_total[..., None] - cumulative)
    read_state = jnp.einsum("ctn,scpn->sctp", c_mat, state_in, precision=highest)
    read_adjoint = jnp.einsum("cin,scpn->scip", b_mat, adjoint_end, precision=highest)
    outputs = head_w[..., None] * read_state + jnp.einsum(
        "scti,scip->sctp", mixed_cb, inputs, precision=highest
    )
    in_grad = (
        jnp.einsum("scti,sctp->scip", mixed_cb, out_grad, precision=highest)
        + tail[..., None] * read_adjoint
    )
    b_part = jnp.einsum("scti,ctn->cin", mixed_gx, c_mat, precision=highest) + jnp.einsum(
        "scip,scpn->cin", tail[..., None] * inputs, adjoint_end, precision=highest
    )
    c_part = jnp.einsum(
        "sctp,scpn->ctn", head_w[..., None] * out_grad, state_in, precision=highest
    ) + jnp.einsum("scti,cin->ctn", mixed_gx, b_mat, precision=highest)
    constant = jnp.exp(span_total) * jnp.sum(adjoint_end * state_in, axis=(-2, -1))
    prior_sum = jnp.einsum(
        "ti,sci->sct", triangle, tail * jnp.sum(inputs * read_adjoint, axis=-1), precision=highest
    )
    later_sum = jnp.einsum(
        "it,sci->sct", triangle, head_w * jnp.sum(out_grad * read_state, axis=-1), precision=highest
    )
    suffix = jnp.einsum("kt,scki->scti", triangle, mixed_gx * cross_cb[None], precision=highest)
    inside_sum = jnp.sum(suffix * triangle, axis=-1)
    decay_part = (
        constant[..., None]
        + prior_sum
        + later_sum
        + inside_sum
        - jnp.sum(in_grad * inputs, axis=-1)
    )
    return (outputs, in_grad, b_part, c_part, decay_part)


def compose(earlier, later):
    return (earlier[0] * later[0], later[0][:, None, None] * earlier[1] + later[1])


def per_device(g_out, w_out, x_act, b_proj, c_proj, log_decay, kept_heads):
    length = x_act.shape[0]
    group = x_act.shape[1] // P_SIZE
    capacity = 3 * kept_heads.shape[0] // (2 * lax.axis_size("head"))
    total_tokens = length * lax.axis_size("ctx")
    spans = length // Q
    head_ids = lax.axis_index("head") * group + jnp.arange(group, dtype=jnp.int32)
    kept_flag = jnp.any(kept_heads[:, None] == head_ids[None, :], axis=0)
    slot_index = jnp.cumsum(kept_flag.astype(jnp.int32)) - 1
    selector = (
        (slot_index[None, :] == jnp.arange(capacity, dtype=jnp.int32)[:, None]) & kept_flag[None, :]
    ).astype(jnp.float32)
    g_whole = lax.all_gather(g_out, "head", axis=1, tiled=True)
    inputs = jnp.einsum(
        "kh,lhp->klp",
        selector,
        x_act.reshape(length, group, P_SIZE).astype(jnp.float32),
        precision=highest,
    ).reshape(capacity, spans, Q, P_SIZE)
    decays = jnp.dot(selector, log_decay, precision=highest).reshape(capacity, spans, Q)
    b_mat = b_proj.astype(jnp.float32).reshape(spans, Q, N)
    c_mat = c_proj.astype(jnp.float32).reshape(spans, Q, N)
    cumulative = jnp.cumsum(decays, axis=-1)
    span_total = cumulative[..., -1]
    before = jnp.exp(jnp.cumsum(span_total, axis=1) - span_total)
    after = jnp.exp(jnp.sum(span_total, axis=1, keepdims=True) - jnp.cumsum(span_total, axis=1))
    device_decay = jnp.exp(jnp.sum(span_total, axis=1))
    identity = (jnp.ones((capacity,), jnp.float32), jnp.zeros((capacity, P_SIZE, N), jnp.float32))
    column = g_whole
    dense = jnp.dot(
        column, lax.all_gather(w_out, "ctx", axis=0, tiled=True), preferred_element_type=jnp.float32
    ).astype(jnp.bfloat16)
    picked = jnp.einsum(
        "kh,lhp->klp",
        selector,
        dense.reshape(length, group, P_SIZE).astype(jnp.float32),
        precision=highest,
    )
    out_grad = picked.reshape(capacity, spans, Q, P_SIZE)
    closing, entering = fold_forward(span_total, state_terms(cumulative, span_total, inputs, b_mat))
    carried = entering_2((device_decay, closing), "ctx", compose, identity, False)
    state_in = entering + before[..., None, None] * carried[1][:, None]
    opening, ending = fold_backward(span_total, adjoint_terms(cumulative, out_grad, c_mat))
    carried_back = entering_2((device_decay, opening), "ctx", compose, identity, True)
    adjoint_end = ending + after[..., None, None] * carried_back[1][:, None]
    outputs, in_grad, b_part, c_part, decay_part = span_outputs(
        cumulative, span_total, inputs, b_mat, c_mat, out_grad, state_in, adjoint_end
    )
    summed = (
        lax.psum(b_part.reshape(length, N).astype(jnp.bfloat16), "head").astype(jnp.float32),
        lax.psum(c_part.reshape(length, N).astype(jnp.bfloat16), "head").astype(jnp.float32),
    )
    b_grad = summed[0] / math.sqrt(KEPT * P_SIZE)
    c_grad = summed[1] * math.sqrt(N / (KEPT * P_SIZE * total_tokens))
    input_grad = jnp.einsum(
        "kh,klp->lhp", selector, in_grad.reshape(capacity, length, P_SIZE), precision=highest
    )
    input_grad = input_grad.astype(jnp.bfloat16).reshape(length, group * P_SIZE)
    decay_grad = jnp.dot(
        selector.T, decay_part.reshape(capacity, length), precision=highest
    ) / math.sqrt(P_SIZE * total_tokens)
    y_kept = outputs.reshape(capacity, length, P_SIZE)
    scale = 1.0 / math.sqrt(total_tokens)
    y_whole = (
        jnp.einsum("kh,klp->lhp", selector, y_kept, precision=highest)
        .astype(jnp.bfloat16)
        .reshape(length, group * P_SIZE)
    )
    column = g_whole
    weight_grad = lax.psum_scatter(
        (jnp.dot(column.T, y_whole, preferred_element_type=jnp.float32) * scale).astype(
            jnp.bfloat16
        ),
        "ctx",
        scatter_dimension=0,
        tiled=True,
    )
    return (input_grad, b_grad, c_grad, decay_grad, weight_grad)


def solution(mesh):
    in_specs = (
        P("ctx", "head"),
        P("ctx", "head"),
        P("ctx", "head"),
        P("ctx", None),
        P("ctx", None),
        P("head", "ctx"),
        P(),
    )
    out_specs = (
        P("ctx", "head"),
        P("ctx", None),
        P("ctx", None),
        P("head", "ctx"),
        P("ctx", "head"),
    )
    return jax.shard_map(
        per_device, mesh=mesh, in_specs=in_specs, out_specs=out_specs, check_vma=False
    )
```

profile of v0, /device:TPU:1, one launch (start us, length us, event | category | flops | bytes accessed | tf_op | source)
XLA Modules:
  0.0 500.6 jit_solution(338513057561109520)
XLA Ops:
  13.3 3.4 fusion.50
  16.7 1.4 broadcast.58.clone
  18.0 3.7 while.59
  24.1 39.0 %all-gather.8.cloned.1.call-done = bf16[512,8192]{1,0:T(8,128)(2,1)} async-done(((bf16[512,1024]{1,0:T(8,128)(2,1)}), bf16[512,8192]{1,0:T(8,128)(2,1)}) %all-gather.8.cloned.1.call-update) | async-done | bytes 8388624 | tf_op jit(solution)/shard_map/all_gather | solution.py:140
  63.1 113.4 %all-gather.10.cloned.1.call-done = bf16[8192,1024]{1,0:T(8,128)(2,1)} async-done(((bf16[512,1024]{1,0:T(8,128)(2,1)}), bf16[8192,1024]{1,0:T(8,128)(2,1)}) %all-gather.10.cloned.1.call-update) | async-done | bytes 16777232 | tf_op jit(solution)/shard_map/all_gather | solution.py:158
  176.5 14.8 %convolution_convert_fusion = bf16[512,1024]{1,0:T(8,128)(2,1)S(1)} fusion(bf16[512,8192]{1,0:T(8,128)(2,1)} %all-gather.8.cloned.1.call-done, bf16[8192,1024]{1,0:T(8,128)(2,1)} %all-gather.10.cloned.1.call-done), kind=kOutput, calls=%fused_computation.65 | convolution fusion | flops 8590458880 | bytes 26214400 | tf_op jit(solution)/shard_map/dot_general | solution.py:157
  193.5 4.6 fusion.47
  198.0 1.3 broadcast.58.clone.1
  199.4 7.7 %while.58 = (s32[]{:T(128)}, f32[12,64,128]{2,1,0:T(8,128)S(1)}, f32[4,12,64,128]{3,2,1,0:T(8,128)}, f32[4,12]{1,0:T(4,128)S(1)}, f32[4,12,64,128]{3,2,0,1:T(8,128)}, /*index=5*/s32[]{:T(128)}, s32[]{:T(128)}, s32[]{:T(128)}) while((s32[]{:T(128)}, f32[12,64,128]{2,1,0:T(8,128)S(1)}, f32[4,12,64,128]{3,2,1,0:T(8,128)}, ...), condition=%wide.region_4.5_spmd.clone, body=%wide.region_3.4_spmd.clone.sunk | while | flops 393220 | bytes 1966352 | solution.py:69
  209.5 31.8 %all-reduce = bf16[192]{0:T(256)(128)(2,1)S(1)} all-reduce(bf16[192]{0:T(256)(128)(2,1)S(1)} %dynamic-update-slice), channel_id=2, replica_groups=mesh['ctx'=16,'head'=8] {'ctx'}, use_global_device_ids=true, to_apply=%add | all-reduce | flops 192 | bytes 768
  242.4 8.8 %fusion.19 = (f32[4,128,128]{2,1,0:T(8,128)S(1)}, f32[12,4,128,128]{3,2,1,0:T(8,128)}) fusion(f32[12,4,128]{2,1,0:T(4,128)S(1)} %copy.231, pred[128,128]{1,0:T(8,128)(4,1)S(1)} %select_compare_fusion, f32[12,4,128,64]{2,0,3,1:T(8,128)} %copy-done.3, f32[12,4,128,64]{2,0,3,1:T(8,128)S(1)} %fusion.83), kind=kOutput, calls=%fused_computation.29 | convolution fusion | flops 607846400 | bytes 6594560 | tf_op jit(solution)/shard_map/sctp,scip->scti/dot_general | solution.py:85
  251.1 25.1 %all-gather.12.cloned.1.call-done = bf16[192,64,128]{2,1,0:T(8,128)(2,1)} async-done(((bf16[12,64,128]{2,1,0:T(8,128)(2,1)}), bf16[192,64,128]{2,1,0:T(8,128)(2,1)}) %all-gather.12.cloned.1.call-update) | async-done | bytes 3145744 | tf_op jit(solution)/shard_map/all_gather | solution.py:22
  276.3 17.0 %while.56 = (s32[]{:T(128)}, f32[12,64,128]{2,1,0:T(8,128)S(1)}, s32[]{:T(128)}, bf16[16,12]{1,0:T(8,128)(2,1)S(1)}, bf16[16,12,64,128]{3,2,1,0:T(8,128)(2,1)}, ...) while((s32[]{:T(128)}, f32[12,64,128]{2,1,0:T(8,128)S(1)}, s32[]{:T(128)}, bf16[16,12]{1,0:T(8,128)(2,1)S(1)}, ...), condition=%wide.region_8.9_spmd, body=%wide.region_7.8_spmd.sunk | while | flops 294930 | bytes 983315 | solution.py:37
  293.3 2.5 multiply_reduce_fusion.1
  295.8 3.0 fusion.70
  298.9 1.5 fusion.20
  300.4 3.0 fusion.65
  303.5 6.6 %fusion.21 = f32[12,4,128,64]{2,3,1,0:T(8,128)S(1)} fusion(f32[4,12,64,128]{3,2,0,1:T(8,128)S(1)} %get-tuple-element.454, f32[4,128,128]{2,1,0:T(8,128)S(1)} %copy-done.16, f32[12,4,128]{2,1,0:T(4,128)S(1)} %copy.231, pred[128,128]{1,0:T(8,128)(4,1)S(1)} %select_compare_fusion, f32[12,4,128]{2,1,0:T(4,128)S(1)} %copy-done.20, ...), kind=kOutput, calls=%fused_computation.33 | convolution fusion | flops 607911936 | bytes 5046272 | tf_op jit(solution)/shard_map/scti,scip->sctp/dot_general | solution.py:92
  310.1 2.2 copy.293
  314.2 2.9 reshape.222
  317.1 2.8 fusion.64
  319.9 1.5 copy.276
  321.5 14.8 %fusion.4 = bf16[8192,1024]{0,1:T(8,128)(2,1)} fusion(bf16[512,1024]{0,1:T(8,128)(2,1)} %bitcast.166, bf16[512,8192]{1,0:T(8,128)(2,1)} %all-gather.8.cloned.1.call-done), kind=kOutput, calls=%fused_computation.15 | convolution fusion | flops 8606711808 | bytes 26214400 | tf_op jit(solution)/shard_map/dot_general | solution.py:198
  336.5 7.8 %fusion.5 = f32[12,4,128]{2,1,0:T(4,128)S(1)} fusion(f32[128,128]{0,1:T(8,128)S(1)} %copy.268, f32[12,4,128,128]{3,2,1,0:T(8,128)} %get-tuple-element.451, f32[4,128,128]{2,1,0:T(8,128)S(1)} %copy-done.16, f32[12,4,128]{2,1,0:T(4,128)S(1)} %copy.231, pred[128,128]{1,0:T(8,128)(4,1)S(1)} %select_compare_fusion), kind=kOutput, calls=%fused_computation.17 | convolution fusion | flops 1213491200 | bytes 3538944 | tf_op jit(solution)/shard_map/kt,scki->scti/dot_general | solution.py:112
  344.5 2.4 fusion.56
  347.0 4.6 multiply_reduce_fusion
  352.0 2.2 copy.289
  354.2 1.9 reshape.220
  360.1 15.9 %all-reduce.4.cloned.1.call-done = (bf16[512,128]{1,0:T(8,128)(2,1)}, bf16[512,128]{1,0:T(8,128)(2,1)}) async-done(((bf16[512,128]{1,0:T(8,128)(2,1)}, bf16[512,128]{1,0:T(8,128)(2,1)}), (bf16[512,128]{1,0:T(8,128)(2,1)}, bf16[512,128]{1,0:T(8,128)(2,1)})) %all-reduce.4.cloned.1.call-update) | async-done | bytes 262160 | tf_op jit(solution)/shard_map/psum | solution.py:177
  376.0 1.8 convert_multiply_fusion
  377.8 113.4 %reduce-scatter.2.cloned.1.call-done = bf16[512,1024]{0,1:T(8,128)(2,1)} async-done(((bf16[8192,1024]{0,1:T(8,128)(2,1)}), bf16[512,1024]{0,1:T(8,128)(2,1)}) %reduce-scatter.2.cloned.1.call-update) | async-done | bytes 1048592 | tf_op jit(solution)/shard_map/reduce_scatter | solution.py:197
  491.2 2.3 copy.278
  (167 shorter events, 47.4 us)
Async XLA Ops:
  7.2 2.1 copy-start
  7.2 1.6 copy-start.21
  7.2 3.8 copy-start.8
  7.2 3.9 copy-start.12
  7.2 55.9 %all-gather.8.cloned.1.call-start = ((), (), s32[]{:S(2)}) async-start(), calls=%async_computation.1 | async-start | bytes 9437184 | tf_op jit(solution)/shard_map/all_gather | solution.py:140
  7.9 168.5 %all-gather.10.cloned.1.call-start = ((), (), s32[]{:S(2)}) async-start(), calls=%async_computation.2 | async-start | bytes 17825792 | tf_op jit(solution)/shard_map/all_gather | solution.py:158
  8.7 233.6 %all-gather.14.cloned.1.call-start = ((), (), s32[]{:S(2)}) async-start(), calls=%async_computation.5 | async-start | bytes 3342336 | tf_op jit(solution)/shard_map/all_gather | solution.py:22
  10.7 1.3 copy-start.10
  11.0 0.9 copy-start.14
  11.0 2.2 copy-start.17
  13.3 4.8 copy-start.3
  18.0 5.3 %copy-start.6 = (bf16[512,128]{1,0:T(8,128)(2,1)S(1)}, bf16[512,128]{1,0:T(8,128)(2,1)}, u32[]{:S(2)}) copy-start(bf16[512,128]{1,0:T(8,128)(2,1)} %param.19) | copy-start | bytes 393220
  22.5 253.8 %all-gather.12.cloned.1.call-start = ((), (), s32[]{:S(2)}) async-start(), calls=%async_computation.4 | async-start | bytes 3342336 | tf_op jit(solution)/shard_map/all_gather | solution.py:22
  192.1 1.3 copy-start.13
  192.1 1.3 copy-start.19
  199.4 8.5 %copy-start.11 = (f32[12,4,128]{2,0,1:T(8,128)S(1)}, f32[12,4,128]{2,0,1:T(8,128)}, u32[]{:S(2)}) copy-start(f32[12,4,128]{2,0,1:T(8,128)} %copy-done.10) | copy-start | bytes 73732
  199.4 8.6 %copy-start.22 = (u32[128]{0:T(128)S(1)}, u32[128]{0:T(128)}, u32[]{:S(2)}) copy-start(u32[128]{0:T(128)} %constant.147) | copy-start | bytes 1540
  199.4 42.0 %copy-start.7 = (bf16[512,128]{1,0:T(8,128)(2,1)S(1)}, bf16[512,128]{1,0:T(8,128)(2,1)}, u32[]{:S(2)}) copy-start(bf16[512,128]{1,0:T(8,128)(2,1)} %param.19) | copy-start | bytes 393220
  199.4 42.0 %copy-start.9 = (bf16[512,128]{1,0:T(8,128)(2,1)S(1)}, bf16[512,128]{1,0:T(8,128)(2,1)}, u32[]{:S(2)}) copy-start(bf16[512,128]{1,0:T(8,128)(2,1)} %param.18) | copy-start | bytes 393220
  207.8 168.2 %all-reduce.4.cloned.1.call-start = ((), (), s32[]{:S(2)}) async-start(), calls=%async_computation.6 | async-start | bytes 524288 | tf_op jit(solution)/shard_map/psum | solution.py:177
  293.3 2.5 copy-start.20
  295.8 4.6 copy-start.2
  298.9 1.6 copy-start.4
  298.9 1.6 copy-start.18
  300.4 3.1 copy-start.16
  321.5 169.7 %reduce-scatter.2.cloned.1.call-start = ((), (), s32[]{:S(2)}) async-start(), calls=%async_computation.3 | async-start | bytes 17825792 | tf_op jit(solution)/shard_map/reduce_scatter | solution.py:197
  344.4 2.6 copy-start.5
  347.0 4.6 copy-start.15
  357.9 135.6 %copy-start.1 = (f32[16,512]{1,0:T(8,128)S(1)}, f32[16,512]{1,0:T(8,128)}, u32[]{:S(2)}) copy-start(f32[16,512]{1,0:T(8,128)} %param.20) | copy-start | bytes 98308
Sparse Core Ops, SparseCore 0:
  9.7 53.3 all-gather.7
  65.2 111.2 all-gather.9
  179.2 47.6 all-gather.13
  229.4 46.7 all-gather.11
  321.6 54.3 all-reduce.3
  379.6 111.5 reduce-scatter.1
where the time goes:
time: 506 us; the launch traced here: 501 us
  waiting for transfers between devices  308 us (61%)
  matrix products  86.3 us (17%)
  other arithmetic  35.7 us (7%)
  blocking collectives  31.8 us (6%)
  local copies, waits for them, and re-layouts  21.3 us (4%)
  between operations  15.6 us (3%)
    reduce_scatter x1, waiting for transfers between devices, per_device(): lax.psum_scatter((jnp.dot(column.T, y_whole, preferred_element_type=jnp.f...  113 us
    all_gather x1, waiting for transfers between devices, per_device(): lax.all_gather(w_out, 'ctx', axis=0, tiled=True)  113 us
    all_gather x1, waiting for transfers between devices, per_device(): g_whole = lax.all_gather(g_out, 'head', axis=1, tiled=True)  39 us
    unnamed x1, blocking collectives  31.8 us
    all_gather x2, waiting for transfers between devices, entering_2(): lax.all_gather(a.astype(kind), axis)  25.1 us
    add x15, other arithmetic, compose(): later[0][:, None, None] * earlier[1] + later[1]  16 us
    psum x1, waiting for transfers between devices, per_device(): lax.psum(b_part.reshape(length, N).astype(jnp.bfloat16), 'head')  15.9 us
    dot_general x1, matrix products, per_device(): jnp.dot(column.T, y_whole, preferred_element_type=jnp.float32) * scale  14.8 us
  transfers between devices with their start and end apart: 6, of which 5 were waited for; matrix products, arithmetic and copies ran while one was open for 19% of the time, Pallas kernels for 0%

commit v1 on v0

v1 whole, which is shorter than its diff:
```python
import math

import jax
import jax.numpy as jnp
from jax import lax
from jax.experimental import pallas as pl
from jax.experimental.pallas import tpu as pltpu
from jax.sharding import PartitionSpec as P

D = 8192
P_SIZE = 64
N = 128
KEPT = 64
Q = 128
TOK = 512
SPANS = TOK // Q
GROUP = 16
CAP = 12
COLS = CAP * P_SIZE
WIDE = GROUP * P_SIZE
PAIRS = CAP // 2
N_CTX = 16
N_HEAD = 8

F32 = jnp.float32
BF = jnp.bfloat16
HIGH = lax.Precision.HIGHEST
MESH = pl.DeviceIdType.MESH
NN = (((1,), (0,)), ((), ()))
NT = (((1,), (1,)), ((), ()))
TN = (((0,), (0,)), ((), ()))


def dot(a, b, dims=NN, precision=None):
    return lax.dot_general(a, b, dims, precision=precision, preferred_element_type=F32)


def rcopy(src, dst, send_sem, recv_sem, device):
    return pltpu.make_async_remote_copy(
        src_ref=src,
        dst_ref=dst,
        send_sem=send_sem,
        recv_sem=recv_sem,
        device_id=device,
        device_id_type=MESH,
    )


def aligned(start, size, unit):
    return pl.ds(pl.multiple_of(start, unit), size)


def loop(lo, hi, body):
    def step(i, carry):
        body(i)
        return carry

    lax.fori_loop(lo, hi, step, 0)


class Gather:
    def __init__(self, block, half, send, recv, me, left, right, device):
        self.block, self.half, self.send, self.recv = block, half, send, recv
        self.me, self.left, self.right = me, left, right
        self.to_left, self.to_right = device(left), device(right)
        self.far = lax.rem(me + 2, 4)

    def copy(self, i):
        ref = (
            lambda: self.block(self.me),
            lambda: self.block(self.me),
            lambda: self.half(self.left, 0),
            lambda: self.half(self.right, 1),
        )[i]()
        return rcopy(ref, ref, self.send(i), self.recv(i), self.to_left if i % 2 else self.to_right)

    def landed(self, slot, ref):
        rcopy(ref, ref, self.send(slot), self.recv(slot), self.to_right).wait_recv()

    def start(self):
        self.copy(0).start()
        self.copy(1).start()

    def forward(self):
        self.landed(0, self.block(self.left))
        self.copy(2).start()
        self.landed(1, self.block(self.right))
        self.copy(3).start()

    def finish(self):
        self.landed(2, self.half(self.far, 0))
        self.landed(3, self.half(self.far, 1))

    def drain(self):
        for i in range(4):
            self.copy(i).wait_send()


class Scatter:
    def __init__(self, term, rows, far, right, left, via_l, via_r, from_l, from_r, own, send, recv, me, device):
        self.term, self.rows, self.h = term, rows, rows // 2
        self.far_buf, self.right_buf, self.left_buf = far, right, left
        self.via_l, self.via_r, self.from_l, self.from_r, self.own = via_l, via_r, from_l, from_r, own
        self.send, self.recv = send, recv
        self.me = me
        self.right, self.left, self.far = lax.rem(me + 1, 4), lax.rem(me + 3, 4), lax.rem(me + 2, 4)
        self.to_right, self.to_left = device(self.right), device(self.left)

    def copy(self, i):
        h = self.h
        lo, hi = pl.ds(0, h), pl.ds(h, h)
        src, dst, to = (
            (self.far_buf.at[lo], self.via_l, self.to_right),
            (self.far_buf.at[hi], self.via_r, self.to_left),
            (self.right_buf.at[hi], self.from_l.at[hi], self.to_right),
            (self.left_buf.at[lo], self.from_r.at[lo], self.to_left),
            (self.right_buf.at[lo], self.from_l.at[lo], self.to_right),
            (self.left_buf.at[hi], self.from_r.at[hi], self.to_left),
        )[i]
        return rcopy(src, dst, self.send.at[i], self.recv.at[i], to)

    def first(self):
        h = self.h
        self.far_buf[:h] = self.term(self.far, 0).astype(BF)
        self.copy(0).start()
        self.far_buf[h:] = self.term(self.far, 1).astype(BF)
        self.copy(1).start()
        self.right_buf[h:] = self.term(self.right, 1).astype(BF)
        self.copy(2).start()
        self.left_buf[:h] = self.term(self.left, 0).astype(BF)
        self.copy(3).start()

    def second(self):
        h = self.h
        self.own[:h] = self.term(self.right, 0)
        self.copy(0).wait_recv()
        self.right_buf[:h] = (self.own[:h] + self.via_l[...].astype(F32)).astype(BF)
        self.copy(4).start()
        self.own[h:] = self.term(self.left, 1)
        self.copy(1).wait_recv()
        self.left_buf[h:] = (self.own[h:] + self.via_r[...].astype(F32)).astype(BF)
        self.copy(5).start()

    def last(self):
        h = self.h
        self.own[:h] = self.term(self.me, 0)
        self.own[h:] = self.term(self.me, 1)

    def finish(self):
        for i in (2, 3, 4, 5):
            self.copy(i).wait_recv()

    def drain(self):
        for i in range(6):
            self.copy(i).wait_send()


class Exchange:
    def __init__(self, source, landed, back, entering, sems, ci, hi):
        self.source, self.landed_ref, self.back, self.entering = source, landed, back, entering
        self.sems, self.ci, self.hi = sems, ci, hi

    def out_copy(self, k, at):
        to = lax.rem(self.ci + k, N_CTX)
        return rcopy(
            self.source.at[aligned(8 * to, 8, 8)],
            self.landed_ref.at[at],
            self.sems.at[0, k],
            self.sems.at[1, k],
            (to, self.hi),
        )

    def back_copy(self, k, at):
        to = lax.rem(self.ci + k, N_CTX)
        return rcopy(
            self.back.at[to],
            self.entering.at[aligned(8 * at, 8, 8)],
            self.sems.at[2, k],
            self.sems.at[3, k],
            (to, self.hi),
        )

    def start(self):
        loop(1, N_CTX, lambda k: self.out_copy(k, self.ci).start())
        self.landed_ref[self.ci] = self.source[aligned(8 * self.ci, 8, 8), :]

    def landed(self):
        loop(1, N_CTX, lambda k: self.out_copy(k, lax.rem(self.ci + N_CTX - k, N_CTX)).wait_recv())

    def reply(self):
        loop(1, N_CTX, lambda k: self.back_copy(k, self.ci).start())
        self.entering[aligned(8 * self.ci, 8, 8), :] = self.back[self.ci]

    def replied(self):
        loop(1, N_CTX, lambda k: self.back_copy(k, lax.rem(self.ci + N_CTX - k, N_CTX)).wait_recv())

    def drain(self):
        def one(k):
            self.out_copy(k, self.ci).wait_send()
            self.back_copy(k, self.ci).wait_send()

        loop(1, N_CTX, one)


def kernel(
    g, w, x, b, c, logd, colidx, headof, sel,
    out_ig, out_b, out_c, out_decay, out_w,
    S, E16, G, W, YT, XS, XT, CUME, CUMR, PART, STIN, YF, YI, L, MS, GK, GH, IG, IGB, SG,
    CFD, RF, EF, ENT, DEC, OPN, RA, EA, AEN, BC, RB, SUM, BCF,
    h_far, h_right, h_left, h_vl, h_vr, h_fl, h_fr, h_own,
    w_far, w_right, w_left, w_vl, w_vr, w_fl, w_fr, w_own,
    loc_sem, a2a_sem, xs_sem, xr_sem, sib_sem, wag_sem, yag_sem, hrs_sem, wrs_sem, fex_sem, bex_sem, bc_sem,
):
    ci, hi = lax.axis_index("ctx"), lax.axis_index("head")
    z, y = ci // 4, lax.rem(ci, 4)
    xx, cc = hi // 2, lax.rem(hi, 2)
    half = y // 2
    cross = lax.rem(half + cc, 2)
    at_x = lambda p: (ci, 2 * p + cc)
    at_y = lambda p: (4 * z + p, hi)
    at_z = lambda p: (4 * p + y, hi)
    sibling = (ci, 2 * xx + 1 - cc)
    nxt = lambda p: lax.rem(p + 1, 4)
    prv = lambda p: lax.rem(p + 3, 4)

    barrier = pltpu.get_barrier_semaphore()

    def greet(device):
        pl.semaphore_signal(barrier, inc=1, device_id=device, device_id_type=MESH)

    loop(1, N_CTX, lambda k: greet((lax.rem(ci + k, N_CTX), hi)))
    loop(1, N_HEAD, lambda k: greet((ci, lax.rem(hi + k, N_HEAD))))

    @pl.when(cross == 1)
    def _():
        for p in range(2):
            greet((4 * z + 2 * cc + p, 2 * xx + 1 - cc))

    def build(i):
        rows = lax.broadcasted_iota(jnp.int32, (128, COLS), 0) + 128 * i
        S[aligned(128 * i, 128, 128), :] = jnp.where(rows == colidx[0:1, :], 1.0, 0.0).astype(BF)

    loop(0, WIDE // 128, build)
    E16[...] = jnp.where(
        lax.broadcasted_iota(jnp.int32, (GROUP, COLS), 0) == headof[0:1, :], 1.0, 0.0
    ).astype(F32)

    def pick_w(i):
        W[aligned(TOK * z + 128 * i, 128, 128), :] = dot(w[aligned(128 * i, 128, 128), :], S[...]).astype(BF)

    loop(0, TOK // 128, pick_w)

    pl.semaphore_wait(barrier, N_CTX - 1 + N_HEAD - 1 + 2 * cross)

    def g_tile(token, feature):
        return G.at[aligned(TOK * token, TOK, TOK), aligned(TOK * feature, TOK, TOK)]

    for p in range(2):
        target = 2 * cc + p
        src = g.at[:, pl.ds(TOK * p, TOK)]

        @pl.when(target == y)
        def _():
            pltpu.make_async_copy(src, g_tile(y, xx), loc_sem.at[0]).start()

        @pl.when(target != y)
        def _():
            rcopy(
                src, g_tile(y, xx), a2a_sem.at[0, p], a2a_sem.at[1, lax.rem(y, 2)], (4 * z + target, 2 * xx + half)
            ).start()

    w_gather = Gather(
        lambda p: W.at[aligned(TOK * p, TOK, TOK), :],
        lambda p, h: W.at[aligned(TOK * p + TOK // 2 * h, TOK // 2, TOK // 2), :],
        lambda i: wag_sem.at[0, i],
        lambda i: wag_sem.at[1, i],
        z, prv(z), nxt(z), at_z,
    )
    w_gather.start()

    sub = lax.broadcasted_iota(jnp.int32, (Q, Q), 0)
    lane = lax.broadcasted_iota(jnp.int32, (Q, Q), 1)
    upto = jnp.where(sub <= lane, 1.0, 0.0).astype(F32)
    below = jnp.where(sub < lane, 1.0, 0.0).astype(F32)
    spread = jnp.where(
        lax.broadcasted_iota(jnp.int32, (128, COLS), 1) // P_SIZE == lax.broadcasted_iota(jnp.int32, (128, COLS), 0),
        1.0,
        0.0,
    ).astype(F32)

    CFD[...] = jnp.zeros_like(CFD)
    DEC[0] = jnp.zeros((8, COLS), F32)

    def local_states(s):
        rows = aligned(Q * s, Q, Q)
        cum = dot(logd[:, rows], upto, precision=HIGH)
        CUMR[:, rows] = dot(sel[...], cum, precision=HIGH)
        cume = dot(cum, E16[...], TN, precision=HIGH)
        CUME[rows, :] = cume
        total = cume[Q - 1 : Q, :]
        xs = dot(x[rows, :], S[...])
        XS[rows, :] = xs.astype(BF)
        xt = (jnp.exp(total - cume) * xs).astype(BF)
        XT[rows, :] = xt
        part = dot(b[rows, :], xt, TN)
        PART[s] = part
        CFD[:, :COLS] = jnp.exp(total) * CFD[:, :COLS] + part
        DEC[0] = DEC[0] + total

    loop(0, SPANS, local_states)
    pick = jnp.where(
        lax.broadcasted_iota(jnp.int32, (COLS, 128), 0) == P_SIZE * lax.broadcasted_iota(jnp.int32, (COLS, 128), 1),
        1.0,
        0.0,
    ).astype(F32)
    totals = dot(DEC[0], pick, precision=HIGH)
    CFD[:, COLS:] = jnp.broadcast_to(totals[0:1, :], (N, 128))
    forward = Exchange(CFD, RF, EF, ENT, fex_sem, ci, hi)
    forward.start()

    x_gathers = []
    for t in range(2):
        token = 2 * cc + t
        x_gathers.append(
            Gather(
                lambda p, token=token: g_tile(token, p),
                lambda p, h, token=token: G.at[
                    aligned(TOK * token + TOK // 2 * h, TOK // 2, TOK // 2), aligned(TOK * p, TOK, TOK)
                ],
                lambda i, t=t: xs_sem.at[t, i],
                lambda i, t=t: xr_sem.at[t, i],
                xx, prv(xx), nxt(xx), at_x,
            )
        )
    ring_x = (xx, prv(xx), nxt(xx), lax.rem(xx + 2, 4))

    def to_sibling(t, j):
        tile = g_tile(2 * cc + t, ring_x[j])
        return rcopy(tile, tile, sib_sem.at[0, t, j], sib_sem.at[1, t, j], sibling)

    def from_sibling(t, j):
        tile = g_tile(2 * (1 - cc) + t, ring_x[j])
        rcopy(tile, tile, sib_sem.at[0, t, j], sib_sem.at[1, t, j], sibling).wait_recv()

    for t in range(2):
        token = 2 * cc + t

        @pl.when(token == y)
        def _():
            pltpu.make_async_copy(g.at[:, pl.ds(0, TOK)], g_tile(token, xx), loc_sem.at[0]).wait()

        @pl.when(token != y)
        def _():
            rcopy(
                g.at[:, pl.ds(0, TOK)], g_tile(token, xx), a2a_sem.at[0, t], a2a_sem.at[1, t], sibling
            ).wait_recv()

        x_gathers[t].start()
        to_sibling(t, 0).start()

    left_half = lane < P_SIZE
    causal = lane <= sub

    def inside(s):
        rows = aligned(Q * s, Q, Q)
        cb = dot(c[rows, :], b[rows, :], NT)
        for k in range(PAIRS):
            cols = pl.ds(Q * k, Q)
            for h in range(2):
                head = 2 * k + h
                differ = CUME[rows, pl.ds(P_SIZE * head, 1)] - CUMR[pl.ds(head, 1), rows]
                low = jnp.where(causal, jnp.exp(jnp.where(causal, differ, 0.0)), 0.0)
                L[PAIRS * s + k, pl.ds(Q * h, Q), :] = low
                MS[PAIRS * s + k, pl.ds(Q * h, Q), :] = (low * cb).astype(BF)
            both = dot(MS[PAIRS * s + k], XS[rows, cols])
            YF[rows, cols] = jnp.where(left_half, both[:Q], both[Q:])

    loop(0, SPANS, inside)

    forward.landed()
    for i in range(N_CTX):
        DEC[i] = jnp.exp(dot(RF[i, :, COLS:], spread, precision=HIGH))
    state = jnp.zeros((8, COLS), F32)
    for i in range(N_CTX):
        EF[i] = state
        state = DEC[i] * state + RF[i, :, :COLS]
    forward.reply()
    w_gather.forward()
    x_gathers[0].forward()
    to_sibling(0, 1).start()
    to_sibling(0, 2).start()
    forward.replied()

    def outputs(s):
        rows = aligned(Q * s, Q, Q)
        cume = CUME[rows, :]
        state_in = ENT[...]
        STIN[s] = state_in
        inter = jnp.exp(cume) * dot(c[rows, :], state_in.astype(BF))
        YI[rows, :] = inter
        whole = YF[rows, :] + inter
        YF[rows, :] = whole
        YT[:, aligned(TOK * y + Q * s, Q, Q)] = whole.T.astype(BF)
        ENT[...] = jnp.exp(cume[Q - 1 : Q, :]) * state_in + PART[s]

    loop(0, SPANS, outputs)
    y_gather = Gather(
        lambda p: YT.at[:, aligned(TOK * p, TOK, TOK)],
        lambda p, h: YT.at[pl.ds(COLS // 2 * h, COLS // 2), aligned(TOK * p, TOK, TOK)],
        lambda i: yag_sem.at[0, i],
        lambda i: yag_sem.at[1, i],
        y, prv(y), nxt(y), at_y,
    )
    y_gather.start()
    x_gathers[1].forward()
    to_sibling(1, 1).start()
    to_sibling(1, 2).start()
    x_gathers[0].finish()
    to_sibling(0, 3).start()
    w_gather.finish()
    x_gathers[1].finish()
    to_sibling(1, 3).start()
    for t in range(2):
        for j in range(4):
            from_sibling(t, j)

    def head_term(block, h):
        return dot(G[aligned(TOK * block + TOK // 2 * h, TOK // 2, TOK // 2), :], W[...])

    def weight_term(block, h):
        return dot(YT[pl.ds(COLS // 2 * h, COLS // 2), :], G[:, aligned(TOK * block, TOK, TOK)])

    heads = Scatter(
        head_term, TOK, h_far, h_right, h_left, h_vl, h_vr, h_fl, h_fr, h_own,
        hrs_sem.at[0], hrs_sem.at[1], y, at_y,
    )
    weights = Scatter(
        weight_term, COLS, w_far, w_right, w_left, w_vl, w_vr, w_fl, w_fr, w_own,
        wrs_sem.at[0], wrs_sem.at[1], z, at_z,
    )
    heads.first()
    y_gather.forward()
    y_gather.finish()
    weights.first()
    heads.second()
    heads.last()
    weights.second()
    weights.last()
    heads.finish()

    def settle(i):
        rows = aligned(128 * i, 128, 128)
        GK[rows, :] = (h_own[rows, :] + h_fl[rows, :].astype(F32) + h_fr[rows, :].astype(F32)).astype(BF)

    loop(0, TOK // 128, settle)

    OPN[...] = jnp.zeros_like(OPN)

    def local_adjoint(i):
        s = SPANS - 1 - i
        rows = aligned(Q * s, Q, Q)
        cume = CUME[rows, :]
        gh = (jnp.exp(cume) * GK[rows, :].astype(F32)).astype(BF)
        GH[rows, :] = gh
        part = dot(c[rows, :], gh, TN)
        PART[s] = part
        OPN[...] = jnp.exp(cume[Q - 1 : Q, :]) * OPN[...] + part

    loop(0, SPANS, local_adjoint)
    backward = Exchange(OPN, RA, EA, AEN, bex_sem, ci, hi)
    backward.start()

    def inside_grad(s):
        rows = aligned(Q * s, Q, Q)
        total = jnp.zeros((Q, Q), F32)
        for k in range(PAIRS):
            cols = pl.ds(Q * k, Q)
            gk = GK[rows, cols].astype(F32)
            stack = jnp.concatenate(
                [jnp.where(left_half, gk, 0.0), jnp.where(left_half, 0.0, gk)], axis=0
            ).astype(BF)
            weighted = L[PAIRS * s + k] * dot(stack, XS[rows, cols], NT)
            total = total + weighted[:Q] + weighted[Q:]
            IG[rows, cols] = dot(MS[PAIRS * s + k], stack, TN)
        SG[s] = total.astype(BF)

    loop(0, SPANS // 2, inside_grad)
    backward.landed()
    state = jnp.zeros((8, COLS), F32)
    for i in reversed(range(N_CTX)):
        EA[i] = state
        state = DEC[i] * state + RA[i]
    backward.reply()
    loop(SPANS // 2, SPANS, inside_grad)
    backward.replied()

    def closing(i):
        s = SPANS - 1 - i
        rows = aligned(Q * s, Q, Q)
        cume = CUME[rows, :]
        total = cume[Q - 1 : Q, :]
        adjoint = AEN[...]
        low = adjoint.astype(BF)
        in_grad = IG[rows, :] + jnp.exp(total - cume) * dot(b[rows, :], low)
        IGB[rows, :] = in_grad.astype(BF)
        sg = SG[s]
        BC[rows, :N] = (dot(sg, c[rows, :], TN) + dot(XT[rows, :], low, NT)).astype(BF)
        BC[rows, N:] = (dot(sg, b[rows, :]) + dot(GH[rows, :], STIN[s].astype(BF), NT)).astype(BF)
        gk = GK[rows, :].astype(F32)
        step = XS[rows, :].astype(F32) * in_grad - gk * YF[rows, :]
        start = jnp.sum(gk * YI[rows, :], axis=0, keepdims=True) + jnp.exp(total) * jnp.sum(
            adjoint * STIN[s], axis=0, keepdims=True
        )
        steps = dot(E16[...], step, NT, precision=HIGH)
        starts = dot(E16[...], jnp.broadcast_to(start, (Q, COLS)), NT, precision=HIGH)
        out_decay[:, rows] = (starts + dot(steps, below, precision=HIGH)) * (1.0 / math.sqrt(P_SIZE * D))
        AEN[...] = jnp.exp(total) * adjoint + PART[s]

    loop(0, SPANS, closing)

    share = TOK // N_HEAD

    def bc_out(k, at):
        to = lax.rem(hi + k, N_HEAD)
        return rcopy(
            BC.at[aligned(share * to, share, share), :], RB.at[at], bc_sem.at[0, k], bc_sem.at[1, k], (ci, to)
        )

    def bc_back(k, at):
        to = lax.rem(hi + k, N_HEAD)
        return rcopy(SUM, BCF.at[aligned(share * at, share, share), :], bc_sem.at[2, k], bc_sem.at[3, k], (ci, to))

    loop(1, N_HEAD, lambda k: bc_out(k, hi).start())
    RB[hi] = BC[aligned(share * hi, share, share), :]

    def spread_in(i):
        rows = aligned(128 * i, 128, 128)
        out_ig[rows, :] = dot(IGB[rows, :], S[...], NT).astype(BF)

    loop(0, TOK // 128, spread_in)
    loop(1, N_HEAD, lambda k: bc_out(k, lax.rem(hi + N_HEAD - k, N_HEAD)).wait_recv())
    summed = RB[0].astype(F32)
    for i in range(1, N_HEAD):
        summed = summed + RB[i].astype(F32)
    SUM[...] = summed.astype(BF)
    BCF[aligned(share * hi, share, share), :] = SUM[...]
    loop(1, N_HEAD, lambda k: bc_back(k, hi).start())

    weights.finish()

    def spread_w(i):
        cols = aligned(128 * i, 128, 128)
        block = (
            (w_own[:, cols] + w_fl[:, cols].astype(F32) + w_fr[:, cols].astype(F32)) * (1.0 / math.sqrt(D))
        ).astype(BF)
        out_w[cols, :] = dot(block, S[...], (((0,), (1,)), ((), ()))).astype(BF)

    loop(0, TOK // 128, spread_w)

    loop(1, N_HEAD, lambda k: bc_back(k, lax.rem(hi + N_HEAD - k, N_HEAD)).wait_recv())
    out_b[...] = BCF[:, :N].astype(F32) / math.sqrt(KEPT * P_SIZE)
    out_c[...] = BCF[:, N:].astype(F32) * math.sqrt(N / (KEPT * P_SIZE * D))

    for p in range(2):

        @pl.when(2 * cc + p != y)
        def _():
            rcopy(
                g.at[:, pl.ds(TOK * p, TOK)], g_tile(y, xx), a2a_sem.at[0, p], a2a_sem.at[1, 0], sibling
            ).wait_send()

    for gather in (w_gather, y_gather, *x_gathers):
        gather.drain()
    for t in range(2):
        for j in range(4):
            to_sibling(t, j).wait_send()
    heads.drain()
    weights.drain()
    forward.drain()
    backward.drain()

    def bc_drain(k):
        bc_out(k, hi).wait_send()
        bc_back(k, hi).wait_send()

    loop(1, N_HEAD, bc_drain)


def per_device(g_out, w_out, x_act, b_proj, c_proj, log_decay, kept_heads):
    head = lax.axis_index("head")
    local = kept_heads - head * GROUP
    mine = (local >= 0) & (local < GROUP)
    rank = jnp.cumsum(mine.astype(jnp.int32)) - 1
    slots = jnp.arange(GROUP, dtype=jnp.int32)
    hit = mine[None, :] & (rank[None, :] == slots[:, None])
    head_of_slot = jnp.sum(jnp.where(hit, local[None, :] + 1, 0), axis=1) - 1
    sel = (head_of_slot[:, None] == slots[None, :]).astype(F32)
    headof = jnp.repeat(head_of_slot[:CAP], P_SIZE)
    colidx = jnp.where(headof >= 0, headof * P_SIZE + jnp.arange(COLS, dtype=jnp.int32) % P_SIZE, -1)
    vmem = pl.BlockSpec(memory_space=pltpu.VMEM)
    buf = pltpu.VMEM
    dma = pltpu.SemaphoreType.DMA

    def ring(rows, cols):
        h = rows // 2
        return [
            buf((rows, cols), BF), buf((rows, cols), BF), buf((rows, cols), BF), buf((h, cols), BF), buf((h, cols), BF),
            buf((rows, cols), BF), buf((rows, cols), BF), buf((rows, cols), F32),
        ]

    return pl.pallas_call(
        kernel,
        out_shape=(
            jax.ShapeDtypeStruct((TOK, WIDE), BF),
            jax.ShapeDtypeStruct((TOK, N), F32),
            jax.ShapeDtypeStruct((TOK, N), F32),
            jax.ShapeDtypeStruct((GROUP, TOK), F32),
            jax.ShapeDtypeStruct((TOK, WIDE), BF),
        ),
        in_specs=[pl.BlockSpec(memory_space=pl.ANY)] + [vmem] * 8,
        out_specs=[vmem] * 5,
        scratch_shapes=[
            buf((WIDE, COLS), BF), buf((GROUP, COLS), F32),
            buf((4 * TOK, 4 * TOK), BF), buf((4 * TOK, COLS), BF), buf((COLS, 4 * TOK), BF),
            buf((TOK, COLS), BF), buf((TOK, COLS), BF), buf((TOK, COLS), F32), buf((GROUP, TOK), F32),
            buf((SPANS, N, COLS), F32), buf((SPANS, N, COLS), F32), buf((TOK, COLS), F32), buf((TOK, COLS), F32),
            buf((SPANS * PAIRS, 2 * Q, Q), F32), buf((SPANS * PAIRS, 2 * Q, Q), BF),
            buf((TOK, COLS), BF), buf((TOK, COLS), BF), buf((TOK, COLS), F32), buf((TOK, COLS), BF),
            buf((SPANS, Q, Q), BF),
            buf((N, COLS + 128), F32), buf((N_CTX, 8, COLS + 128), F32), buf((N_CTX, 8, COLS), F32),
            buf((N, COLS), F32), buf((N_CTX, 8, COLS), F32),
            buf((N, COLS), F32), buf((N_CTX, 8, COLS), F32), buf((N_CTX, 8, COLS), F32), buf((N, COLS), F32),
            buf((TOK, 2 * N), BF), buf((N_HEAD, TOK // N_HEAD, 2 * N), BF), buf((TOK // N_HEAD, 2 * N), BF),
            buf((TOK, 2 * N), BF),
            *ring(TOK, COLS), *ring(COLS, TOK),
            dma((1,)), dma((2, 2)), dma((2, 4)), dma((2, 4)), dma((2, 2, 4)), dma((2, 4)), dma((2, 4)),
            dma((2, 6)), dma((2, 6)), dma((4, N_CTX)), dma((4, N_CTX)), dma((4, N_HEAD)),
        ],
        compiler_params=pltpu.CompilerParams(
            collective_id=0, has_side_effects=True, vmem_limit_bytes=62 * 1024 * 1024
        ),
        cost_estimate=pl.CostEstimate(flops=14_000_000_000, bytes_accessed=8_000_000, transcendentals=4_000_000),
    )(
        g_out, w_out, x_act, b_proj, c_proj, log_decay,
        jnp.broadcast_to(colidx[None, :], (8, COLS)), jnp.broadcast_to(headof[None, :], (8, COLS)), sel,
    )


def solution(mesh):
    in_specs = (
        P("ctx", "head"),
        P("ctx", "head"),
        P("ctx", "head"),
        P("ctx", None),
        P("ctx", None),
        P("head", "ctx"),
        P(),
    )
    out_specs = (
        P("ctx", "head"),
        P("ctx", None),
        P("ctx", None),
        P("head", "ctx"),
        P("ctx", "head"),
    )
    return jax.shard_map(
        per_device, mesh=mesh, in_specs=in_specs, out_specs=out_specs, check_vma=False
    )
```

time: 506 us -> 162 us (0.32); the launches traced: 501 us -> 162 us
  waiting for transfers between devices: 308 us -> 0 us
  Pallas kernels: 0 us -> 153 us
  matrix products: 86.3 us -> 0 us
  other arithmetic: 35.7 us -> 1.02 us
  blocking collectives: 31.8 us -> 0 us
  between operations: 15.6 us -> 0.7 us
  local copies, waits for them, and re-layouts: 21.3 us -> 7.43 us
    all_gather x4 -> x0, waiting for transfers between devices: 178 us -> none  [the longest x1 113 us: per_device(): lax.all_gather(w_out, 'ctx', axis=0, tiled=True)]
    pallas_call x0 -> x1, Pallas kernels: none -> 153 us  [per_device(): pl.pallas_call(kernel, out_shape=(jax.ShapeDtypeStruct((TOK, WIDE), BF),...]
    reduce_scatter x1 -> x0, waiting for transfers between devices: 113 us -> none  [per_device(): lax.psum_scatter((jnp.dot(column.T, y_whole, preferred_element_type=jnp.f...]
    dot_general x23 -> x0, matrix products: 86.3 us -> none  [the longest x1 14.8 us: per_device(): jnp.dot(column.T, y_whole, preferred_element_type=jnp.float32) * scale]
    unnamed x1 -> x0, blocking collectives: 31.8 us -> none
    add x24 -> x1, other arithmetic: 20.8 us -> 0.01 us  [per_device(): head_of_slot = jnp.sum(jnp.where(hit, local[None, :] + 1, 0), axis=1) - 1]
    psum x1 -> x0, waiting for transfers between devices: 15.9 us -> none  [per_device(): lax.psum(b_part.reshape(length, N).astype(jnp.bfloat16), 'head')]
    reshape x6 -> x1, local copies, waits for them, and re-layouts: 9.1 us -> 0.07 us  [per_device(): headof = jnp.repeat(head_of_slot[:CAP], P_SIZE)]
  transfers between devices with their start and end apart: 6 -> 0, of which waited for: 5 -> 0; matrix products, arithmetic and copies ran while one was open for 19% -> 0% of each run, Pallas kernels for 0% -> 0%
where the time goes in v1:
time: 162 us
  Pallas kernels  153 us (94%)
  local copies, waits for them, and re-layouts  7.43 us (5%)
    pallas_call x1, Pallas kernels, per_device(): pl.pallas_call(kernel, out_shape=(jax.ShapeDtypeStruct((TOK, WIDE), BF),...  153 us
    unnamed x15, local copies, waits for them, and re-layouts  5.97 us

profile of v1, /device:TPU:1, one launch (start us, length us, event | category | flops | bytes accessed | tf_op | source)
XLA Modules:
  0.0 161.7 jit_solution(379845813444509139)
XLA Ops:
  0.6 0.0 copy-start.4
  0.6 0.6 copy-done.4
  1.3 0.1 copy.14
  1.4 0.1 reduce-window.8
  1.5 0.1 add_reduce_fusion
  1.6 0.1 select_reduce_fusion
  1.7 0.1 broadcast_in_dim.38
  1.8 0.1 reshape.69
  1.9 0.7 fusion.1.sel
  2.6 0.6 broadcast_in_dim.41.headof
  3.2 0.6 broadcast_in_dim.40.colidx
  3.8 152.6 %shard_map.110 = (bf16[512,1024]{1,0:T(8,128)(2,1)}, f32[512,128]{1,0:T(8,128)}, f32[512,128]{1,0:T(8,128)}, f32[16,512]{1,0:T(8,128)}, bf16[512,1024]{1,0:T(8,128)(2,1)}) custom-call(bf16[512,1024]{1,0:T(8,128)(2,1)} %g.1, bf16[512,1024]{1,0:T(8,128)(2,1)} %w.1, bf16[512,1024]{1,0:T(8,128)(2,1)} %x.1, bf16[512,128]{1,0:T(8,128)(2,1)} %b.1, ...), custom_call_target="tpu_custom_call" | custom-call | flops 14000000000 | bytes 8000000 | tf_op jit(solution)/shard_map/pallas_call | solution.py:611
  156.4 0.0 copy-start.2
  156.4 0.0 copy-start.1
  156.4 0.0 copy-start.3
  156.4 2.3 %copy.20 = bf16[512,1024]{1,0:T(8,128)(2,1)} copy(bf16[512,1024]{1,0:T(8,128)(2,1)} %get-tuple-element.12) | data formatting | bytes 2097152
  158.7 0.0 copy-done.2
  158.7 0.0 copy-start
  158.7 0.7 copy.21
  159.4 0.0 copy-done.1
  159.4 0.7 copy.22
  160.1 0.0 copy-done.3
  160.1 0.6 copy.23
  160.7 0.0 copy-done
  160.7 1.0 copy.24
  (4 shorter events, 0.0 us)
Async XLA Ops:
  0.6 0.7 copy-start.4
  156.4 2.3 %copy-start.2 = (f32[512,128]{1,0:T(8,128)S(1)}, f32[512,128]{1,0:T(8,128)}, u32[]{:S(2)}) copy-start(f32[512,128]{1,0:T(8,128)} %get-tuple-element.13) | copy-start | bytes 786436
  156.4 3.0 %copy-start.1 = (f32[512,128]{1,0:T(8,128)S(1)}, f32[512,128]{1,0:T(8,128)}, u32[]{:S(2)}) copy-start(f32[512,128]{1,0:T(8,128)} %get-tuple-element.14) | copy-start | bytes 786436
  156.4 3.7 %copy-start.3 = (f32[16,512]{1,0:T(8,128)S(1)}, f32[16,512]{1,0:T(8,128)}, u32[]{:S(2)}) copy-start(f32[16,512]{1,0:T(8,128)} %get-tuple-element.15) | copy-start | bytes 98308
  158.7 2.0 %copy-start = (bf16[512,1024]{1,0:T(8,128)(2,1)S(1)}, bf16[512,1024]{1,0:T(8,128)(2,1)}, u32[]{:S(2)}) copy-start(bf16[512,1024]{1,0:T(8,128)(2,1)} %get-tuple-element.16) | copy-start | bytes 3145732

commit v2 on v1

v2 whole, which is shorter than its diff:
```python
import math

import jax
import jax.numpy as jnp
from jax import lax
from jax.experimental import pallas as pl
from jax.experimental.pallas import tpu as pltpu
from jax.sharding import PartitionSpec as P

D = 8192
P_SIZE = 64
N = 128
KEPT = 64
Q = 128
TOK = 512
SPANS = TOK // Q
GROUP = 16
CAP = 12
COLS = CAP * P_SIZE
WIDE = GROUP * P_SIZE
PAIRS = CAP // 2
N_CTX = 16
N_HEAD = 8
HALF = COLS // 2
VMEM_LIMIT = 62 * 1024 * 1024

F32 = jnp.float32
BF = jnp.bfloat16
HIGH = lax.Precision.HIGHEST
MESH = pl.DeviceIdType.MESH
NN = (((1,), (0,)), ((), ()))
NT = (((1,), (1,)), ((), ()))
TN = (((0,), (0,)), ((), ()))


def dot(a, b, dims=NN, precision=None):
    return lax.dot_general(a, b, dims, precision=precision, preferred_element_type=F32)


def rcopy(src, dst, send_sem, recv_sem, device):
    return pltpu.make_async_remote_copy(
        src_ref=src,
        dst_ref=dst,
        send_sem=send_sem,
        recv_sem=recv_sem,
        device_id=device,
        device_id_type=MESH,
    )


def aligned(start, size, unit):
    return pl.ds(pl.multiple_of(start, unit), size)


def loop(lo, hi, body):
    def step(i, carry):
        body(i)
        return carry

    lax.fori_loop(lo, hi, step, 0)


class Gather:
    def __init__(self, block, half, send, recv, me, left, right, device):
        self.block, self.half, self.send, self.recv = block, half, send, recv
        self.me, self.left, self.right = me, left, right
        self.to_left, self.to_right = device(left), device(right)
        self.far = lax.rem(me + 2, 4)

    def copy(self, i):
        ref = (
            lambda: self.block(self.me),
            lambda: self.block(self.me),
            lambda: self.half(self.left, 0),
            lambda: self.half(self.right, 1),
        )[i]()
        return rcopy(ref, ref, self.send(i), self.recv(i), self.to_left if i % 2 else self.to_right)

    def landed(self, slot, ref):
        rcopy(ref, ref, self.send(slot), self.recv(slot), self.to_right).wait_recv()

    def start(self):
        self.copy(0).start()
        self.copy(1).start()

    def forward(self):
        self.landed(0, self.block(self.left))
        self.copy(2).start()
        self.landed(1, self.block(self.right))
        self.copy(3).start()

    def finish(self):
        self.landed(2, self.half(self.far, 0))
        self.landed(3, self.half(self.far, 1))

    def drain(self):
        for i in range(4):
            self.copy(i).wait_send()


class Scatter:
    def __init__(self, term, rows, far, right, left, via_l, via_r, from_l, from_r, own, send, recv, me, device):
        self.term, self.h = term, rows // 2
        self.far_buf, self.right_buf, self.left_buf = far, right, left
        self.via_l, self.via_r, self.from_l, self.from_r, self.own = via_l, via_r, from_l, from_r, own
        self.send, self.recv = send, recv
        self.me = me
        self.right, self.left, self.far = lax.rem(me + 1, 4), lax.rem(me + 3, 4), lax.rem(me + 2, 4)
        self.to_right, self.to_left = device(self.right), device(self.left)

    def copy(self, i):
        lo, hi = pl.ds(0, self.h), pl.ds(self.h, self.h)
        src, dst, to = (
            (self.far_buf.at[lo], self.via_l, self.to_right),
            (self.far_buf.at[hi], self.via_r, self.to_left),
            (self.right_buf.at[hi], self.from_l.at[hi], self.to_right),
            (self.left_buf.at[lo], self.from_r.at[lo], self.to_left),
            (self.right_buf.at[lo], self.from_l.at[lo], self.to_right),
            (self.left_buf.at[hi], self.from_r.at[hi], self.to_left),
        )[i]
        return rcopy(src, dst, self.send.at[i], self.recv.at[i], to)

    def first(self):
        h = self.h
        self.far_buf[...] = self.term(self.far).astype(BF)
        self.copy(0).start()
        self.copy(1).start()
        term = self.term(self.right)
        self.right_buf[h:] = term[h:].astype(BF)
        self.copy(2).start()
        self.own[:h] = term[:h]
        term = self.term(self.left)
        self.left_buf[:h] = term[:h].astype(BF)
        self.copy(3).start()
        self.own[h:] = term[h:]

    def second(self):
        h = self.h
        self.copy(0).wait_recv()
        self.right_buf[:h] = (self.own[:h] + self.via_l[...].astype(F32)).astype(BF)
        self.copy(4).start()
        self.copy(1).wait_recv()
        self.left_buf[h:] = (self.own[h:] + self.via_r[...].astype(F32)).astype(BF)
        self.copy(5).start()

    def last(self):
        self.own[...] = self.term(self.me)

    def finish(self):
        for i in (2, 3, 4, 5):
            self.copy(i).wait_recv()

    def result(self, rows, cols=slice(None)):
        return self.own[rows, cols] + self.from_l[rows, cols].astype(F32) + self.from_r[rows, cols].astype(F32)

    def drain(self):
        for i in range(6):
            self.copy(i).wait_send()


class Exchange:
    def __init__(self, source, landed, back, entering, sems, ci, hi):
        self.source, self.landed_ref, self.back, self.entering = source, landed, back, entering
        self.sems, self.ci, self.hi = sems, ci, hi

    def cut(self, r):
        return aligned(16 * (r // 2), 16, 16), aligned(HALF * lax.rem(r, 2), HALF, 128)

    def slot(self, r):
        return aligned(16 * r, 16, 16)

    def out_copy(self, k, at):
        to = lax.rem(self.ci + k, N_CTX)
        return rcopy(
            self.source.at[self.cut(to)], self.landed_ref.at[self.slot(at), :],
            self.sems.at[0, k], self.sems.at[1, k], (to, self.hi),
        )

    def back_copy(self, k, at):
        to = lax.rem(self.ci + k, N_CTX)
        return rcopy(
            self.back.at[self.slot(to), :], self.entering.at[self.cut(at)],
            self.sems.at[2, k], self.sems.at[3, k], (to, self.hi),
        )

    def start(self):
        loop(1, N_CTX, lambda k: self.out_copy(k, self.ci).start())
        self.landed_ref[self.slot(self.ci), :] = self.source[self.cut(self.ci)]

    def landed(self):
        loop(1, N_CTX, lambda k: self.out_copy(k, lax.rem(self.ci + N_CTX - k, N_CTX)).wait_recv())

    def scan(self, decays, order):
        state = jnp.zeros((16, HALF), F32)
        for i in order:
            rows = pl.ds(16 * i, 16)
            self.back[rows, :] = state.astype(BF)
            state = decays[pl.ds(8 * i, 1), :] * state + self.landed_ref[rows, :].astype(F32)

    def reply(self):
        loop(1, N_CTX, lambda k: self.back_copy(k, self.ci).start())
        self.entering[self.cut(self.ci)] = self.back[self.slot(self.ci), :]

    def replied(self):
        loop(1, N_CTX, lambda k: self.back_copy(k, lax.rem(self.ci + N_CTX - k, N_CTX)).wait_recv())

    def drain(self):
        def one(k):
            self.out_copy(k, self.ci).wait_send()
            self.back_copy(k, self.ci).wait_send()

        loop(1, N_CTX, one)


class HeadSum:
    def __init__(self, part, landed, total, whole, sems, ci, hi):
        self.part, self.landed_ref, self.total, self.whole = part, landed, total, whole
        self.sems, self.ci, self.hi = sems, ci, hi

    def share(self, r):
        return aligned(TOK // N_HEAD * r, TOK // N_HEAD, TOK // N_HEAD)

    def out_copy(self, k, at):
        to = lax.rem(self.hi + k, N_HEAD)
        return rcopy(
            self.part.at[self.share(to), :], self.landed_ref.at[at],
            self.sems.at[0, k], self.sems.at[1, k], (self.ci, to),
        )

    def back_copy(self, k, at):
        to = lax.rem(self.hi + k, N_HEAD)
        return rcopy(
            self.total, self.whole.at[self.share(at), :], self.sems.at[2, k], self.sems.at[3, k], (self.ci, to)
        )

    def start(self):
        loop(1, N_HEAD, lambda k: self.out_copy(k, self.hi).start())
        self.landed_ref[self.hi] = self.part[self.share(self.hi), :]

    def reduce(self):
        loop(1, N_HEAD, lambda k: self.out_copy(k, lax.rem(self.hi + N_HEAD - k, N_HEAD)).wait_recv())
        total = self.landed_ref[0].astype(F32)
        for i in range(1, N_HEAD):
            total = total + self.landed_ref[i].astype(F32)
        self.total[...] = total.astype(BF)
        loop(1, N_HEAD, lambda k: self.back_copy(k, self.hi).start())
        self.whole[self.share(self.hi), :] = self.total[...]

    def finish(self):
        loop(1, N_HEAD, lambda k: self.back_copy(k, lax.rem(self.hi + N_HEAD - k, N_HEAD)).wait_recv())

    def drain(self):
        def one(k):
            self.out_copy(k, self.hi).wait_send()
            self.back_copy(k, self.hi).wait_send()

        loop(1, N_HEAD, one)


def one_hot(rows, cols, hit):
    r = lax.broadcasted_iota(jnp.int32, (rows, cols), 0)
    k = lax.broadcasted_iota(jnp.int32, (rows, cols), 1)
    return jnp.where(hit(r, k), 1.0, 0.0).astype(F32)


def kernel(
    kept, g, w_in, x_in, b_in, c_in, logd_in,
    out_ig, out_b, out_c, out_decay, out_w,
    w, x, b, c, logd, S, E16, E16B, G, W, YT, XS, XT, CUME, CUMR, PART, STIN, ADJ, YF, YI, L, MS, GK, GH, IG, IGB, B0,
    TOT, RD, DEC, ST, FL, FB, FE, AL, AB, AE, BP, BL, BT, BW, CP, CL, CT, CW, O_IG, O_B, O_C, O_D, O_W,
    a_far, a_right, a_left, a_vl, a_vr, a_fl, a_fr, a_own,
    b_far, b_right, b_left, b_vl, b_vr, b_fl, b_fr, b_own,
    w_far, w_right, w_left, w_vl, w_vr, w_fl, w_fr, w_own,
    loc_sem, own_sem, a2a_sem, xs_sem, xr_sem, sib_sem, wag_sem, yag_sem, hrs_sem, wrs_sem, dec_sem, fex_sem, bex_sem,
    b_sem, c_sem, out_sem,
):
    ci, hi = lax.axis_index("ctx"), lax.axis_index("head")
    z, y = ci // 4, lax.rem(ci, 4)
    xx, cc = hi // 2, lax.rem(hi, 2)
    half = y // 2
    cross = lax.rem(half + cc, 2)
    at_x = lambda p: (ci, 2 * p + cc)
    at_y = lambda p: (4 * z + p, hi)
    at_z = lambda p: (4 * p + y, hi)
    sibling = (ci, 2 * xx + 1 - cc)
    nxt = lambda p: lax.rem(p + 1, 4)
    prv = lambda p: lax.rem(p + 3, 4)

    barrier = pltpu.get_barrier_semaphore()

    def greet(device):
        pl.semaphore_signal(barrier, inc=1, device_id=device, device_id_type=MESH)

    loop(1, N_CTX, lambda k: greet((lax.rem(ci + k, N_CTX), hi)))
    loop(1, N_HEAD, lambda k: greet((ci, lax.rem(hi + k, N_HEAD))))

    @pl.when(cross == 1)
    def _():
        for p in range(2):
            greet((4 * z + 2 * cc + p, 2 * xx + 1 - cc))

    loads = [
        pltpu.make_async_copy(src, dst, loc_sem.at[i])
        for i, (src, dst) in enumerate(((w_in, w), (x_in, x), (b_in, b), (c_in, c), (logd_in, logd)))
    ]
    for load in loads:
        load.start()

    lanes = lax.broadcasted_iota(jnp.int32, (8, COLS), 1)

    def place(k, carry):
        headof, rank = carry
        local = kept[k] - GROUP * hi
        mine = (local >= 0) & (local < GROUP)
        headof = jnp.where(lanes // P_SIZE == jnp.where(mine, rank, -1), local, headof)
        return headof, rank + jnp.where(mine, 1, 0)

    headof, _ = lax.fori_loop(0, KEPT, place, (jnp.full((8, COLS), -1, jnp.int32), jnp.int32(0)))
    headof = headof[0:1, :]
    colidx = jnp.where(headof >= 0, P_SIZE * headof + lax.rem(lanes[0:1, :], P_SIZE), -1)

    def build(i):
        rows = lax.broadcasted_iota(jnp.int32, (128, COLS), 0) + 128 * i
        S[aligned(128 * i, 128, 128), :] = jnp.where(rows == colidx, 1.0, 0.0).astype(BF)

    loop(0, WIDE // 128, build)
    E16[...] = jnp.where(lax.broadcasted_iota(jnp.int32, (GROUP, COLS), 0) == headof, 1.0, 0.0).astype(F32)
    E16B[...] = E16[...].astype(BF)

    pl.semaphore_wait(barrier, N_CTX - 1 + N_HEAD - 1 + 2 * cross)

    def g_tile(token, feature, q):
        return G.at[token, :, q, :, aligned(TOK * feature, TOK, TOK)]

    def quarter(q, p):
        return g.at[:, q, :, pl.ds(TOK * p, TOK)]

    def a2a_copy(q, p, slot):
        return rcopy(
            quarter(q, p), g_tile(y, xx, q), a2a_sem.at[0, q, p], a2a_sem.at[1, q, slot], (4 * z + 2 * cc + p, 2 * xx + half)
        )

    def a2a_start(q):
        for p in range(2):

            @pl.when(2 * cc + p == y)
            def _():
                pltpu.make_async_copy(quarter(q, p), g_tile(y, xx, q), own_sem.at[q]).start()

            @pl.when(2 * cc + p != y)
            def _():
                a2a_copy(q, p, lax.rem(y, 2)).start()

    def a2a_landed(q, t):
        token = 2 * cc + t

        @pl.when(token == y)
        def _():
            pltpu.make_async_copy(quarter(q, 0), g_tile(token, xx, q), own_sem.at[q]).wait()

        @pl.when(token != y)
        def _():
            rcopy(
                quarter(q, 0), g_tile(token, xx, q), a2a_sem.at[0, q, t], a2a_sem.at[1, q, t], sibling
            ).wait_recv()

    a2a_start(0)

    for load in loads:
        load.wait()

    def pick_w(i):
        W[aligned(TOK * z + 128 * i, 128, 128), :] = dot(w[aligned(128 * i, 128, 128), :], S[...]).astype(BF)

    loop(0, TOK // 128, pick_w)
    w_gather = Gather(
        lambda p: W.at[aligned(TOK * p, TOK, TOK), :],
        lambda p, h: W.at[aligned(TOK * p + TOK // 2 * h, TOK // 2, TOK // 2), :],
        lambda i: wag_sem.at[0, i],
        lambda i: wag_sem.at[1, i],
        z, prv(z), nxt(z), at_z,
    )
    w_gather.start()

    upto = one_hot(Q, Q, lambda r, k: r <= k)
    pick = one_hot(COLS, 128, lambda r, k: r == P_SIZE * k)
    slots = dot(E16[...], pick)[:, :GROUP]

    def decays(s):
        rows = aligned(Q * s, Q, Q)
        cum = dot(logd[:, rows], upto, precision=HIGH)
        CUMR[:, rows] = dot(slots, cum, TN, precision=HIGH)
        CUME[rows, :] = dot(cum, E16[...], TN, precision=HIGH)

    loop(0, SPANS, decays)
    totals = sum(CUMR[:, pl.ds(Q * s + Q - 1, 1)] for s in range(SPANS))
    TOT[...] = dot(jnp.broadcast_to(totals, (GROUP, 8)), one_hot(GROUP, 128, lambda r, k: r == k), TN, precision=HIGH)

    def decay_copy(k, at):
        to = lax.rem(ci + k, N_CTX)
        return rcopy(TOT, RD.at[aligned(8 * at, 8, 8), :], dec_sem.at[0, k], dec_sem.at[1, k], (to, hi))

    loop(1, N_CTX, lambda k: decay_copy(k, ci).start())
    RD[aligned(8 * ci, 8, 8), :] = TOT[...]

    STIN[0] = jnp.zeros((N, COLS), F32)

    def local_states(s):
        rows = aligned(Q * s, Q, Q)
        cume = CUME[rows, :]
        total = cume[Q - 1 : Q, :]
        xs = dot(x[rows, :], S[...])
        XS[rows, :] = xs.astype(BF)
        xt = (jnp.exp(total - cume) * xs).astype(BF)
        XT[rows, :] = xt
        part = dot(b[rows, :], xt, TN)
        PART[s] = part
        STIN[0] = jnp.exp(total) * STIN[0] + part

    loop(0, SPANS, local_states)
    ST[0] = STIN[0].astype(BF)
    forward = Exchange(ST.at[0], FL, FB, FE, fex_sem, ci, hi)
    forward.start()

    def x_gather(q, t):
        token = 2 * cc + t
        return Gather(
            lambda p: g_tile(token, p, q),
            lambda p, h: G.at[token, h, q, :, aligned(TOK * p, TOK, TOK)],
            lambda i: xs_sem.at[q, t, i],
            lambda i: xr_sem.at[q, t, i],
            xx, prv(xx), nxt(xx), at_x,
        )

    x_gathers = [[x_gather(q, t) for t in range(2)] for q in range(2)]
    ring_x = (xx, prv(xx), nxt(xx), lax.rem(xx + 2, 4))

    def sibling_copy(q, t, j, core):
        tile = g_tile(2 * core + t, ring_x[j], q)
        return rcopy(tile, tile, sib_sem.at[0, q, t, j], sib_sem.at[1, q, t, j], sibling)

    def x_start(q):
        for t in range(2):
            a2a_landed(q, t)
            x_gathers[q][t].start()
            sibling_copy(q, t, 0, cc).start()

    def x_forward(q):
        for t in range(2):
            x_gathers[q][t].forward()
            sibling_copy(q, t, 1, cc).start()
            sibling_copy(q, t, 2, cc).start()

    def x_finish(q):
        for t in range(2):
            x_gathers[q][t].finish()
            sibling_copy(q, t, 3, cc).start()
        for t in range(2):
            for j in range(4):
                sibling_copy(q, t, j, 1 - cc).wait_recv()

    x_start(0)
    a2a_start(1)

    sub = lax.broadcasted_iota(jnp.int32, (Q, Q), 0)
    lane = lax.broadcasted_iota(jnp.int32, (Q, Q), 1)
    left_half = lane < P_SIZE
    causal = lane <= sub

    def inside(s):
        rows = aligned(Q * s, Q, Q)
        cb = dot(c[rows, :], b[rows, :], NT)
        for k in range(PAIRS):
            cols = pl.ds(Q * k, Q)
            for h in range(2):
                head = 2 * k + h
                differ = CUME[rows, pl.ds(P_SIZE * head, 1)] - CUMR[pl.ds(head, 1), rows]
                low = jnp.where(causal, jnp.exp(jnp.where(causal, differ, 0.0)), 0.0)
                L[PAIRS * s + k, pl.ds(Q * h, Q), :] = low
                MS[PAIRS * s + k, pl.ds(Q * h, Q), :] = (low * cb).astype(BF)
            both = dot(MS[PAIRS * s + k], XS[rows, cols])
            YF[rows, cols] = jnp.where(left_half, both[:Q], both[Q:])

    loop(0, SPANS, inside)

    loop(1, N_CTX, lambda k: decay_copy(k, lax.rem(ci + N_CTX - k, N_CTX)).wait_recv())
    first_slot = CAP // 2 * lax.rem(ci, 2)
    DEC[...] = jnp.exp(dot(RD[...], one_hot(128, HALF, lambda r, k: r == k // P_SIZE + first_slot), precision=HIGH))
    forward.landed()
    forward.scan(DEC, range(N_CTX))
    forward.reply()
    w_gather.forward()
    forward.replied()
    STIN[0] = FE[...].astype(F32)

    def outputs(s):
        rows = aligned(Q * s, Q, Q)
        cume = CUME[rows, :]
        state_in = STIN[s]
        inter = jnp.exp(cume) * dot(c[rows, :], state_in.astype(BF))
        YI[rows, :] = inter
        whole = YF[rows, :] + inter
        YF[rows, :] = whole
        YT[:, aligned(TOK * y + Q * s, Q, Q)] = whole.T.astype(BF)
        STIN[s + 1] = jnp.exp(cume[Q - 1 : Q, :]) * state_in + PART[s]

    loop(0, SPANS, outputs)
    y_gather = Gather(
        lambda p: YT.at[:, aligned(TOK * p, TOK, TOK)],
        lambda p, h: YT.at[pl.ds(HALF * h, HALF), aligned(TOK * p, TOK, TOK)],
        lambda i: yag_sem.at[0, i],
        lambda i: yag_sem.at[1, i],
        y, prv(y), nxt(y), at_y,
    )
    y_gather.start()

    def head_term(q):
        return lambda block: dot(G[block, :, q].reshape(TOK // 2, 4 * TOK), W[...])

    def weight_term(block):
        return dot(YT[...], G[:, :, :, :, aligned(TOK * block, TOK, TOK)].reshape(4 * TOK, TOK))

    heads = (
        Scatter(
            head_term(0), TOK // 2, a_far, a_right, a_left, a_vl, a_vr, a_fl, a_fr, a_own,
            hrs_sem.at[0, 0], hrs_sem.at[0, 1], y, at_y,
        ),
        Scatter(
            head_term(1), TOK // 2, b_far, b_right, b_left, b_vl, b_vr, b_fl, b_fr, b_own,
            hrs_sem.at[1, 0], hrs_sem.at[1, 1], y, at_y,
        ),
    )
    weights = Scatter(
        weight_term, COLS, w_far, w_right, w_left, w_vl, w_vr, w_fl, w_fr, w_own,
        wrs_sem.at[0], wrs_sem.at[1], z, at_z,
    )

    def local_adjoint(s):
        rows = pl.ds(Q * s, Q)
        GK[rows, :] = heads[s % 2].result(pl.ds(Q * (s // 2), Q)).astype(BF)
        gh = (jnp.exp(CUME[rows, :]) * GK[rows, :].astype(F32)).astype(BF)
        GH[rows, :] = gh
        PART[s] = dot(c[rows, :], gh, TN)

    def inside_grad(s):
        rows = aligned(Q * s, Q, Q)
        total = jnp.zeros((Q, Q), F32)
        for k in range(PAIRS):
            cols = pl.ds(Q * k, Q)
            gk = GK[rows, cols].astype(F32)
            stack = jnp.concatenate(
                [jnp.where(left_half, gk, 0.0), jnp.where(left_half, 0.0, gk)], axis=0
            ).astype(BF)
            weighted = L[PAIRS * s + k] * dot(stack, XS[rows, cols], NT)
            total = total + weighted[:Q] + weighted[Q:]
            IG[rows, cols] = dot(MS[PAIRS * s + k], stack, TN)
        sg = total.astype(BF)
        B0[rows, :] = dot(sg, c[rows, :], TN)
        CP[rows, :] = (dot(sg, b[rows, :]) + dot(GH[rows, :], STIN[s].astype(BF), NT)).astype(BF)

    x_forward(0)
    x_start(1)
    w_gather.finish()
    x_finish(0)
    heads[0].first()
    x_forward(1)
    y_gather.forward()
    heads[0].second()
    heads[0].last()
    x_finish(1)
    heads[1].first()
    heads[0].finish()
    local_adjoint(0)
    local_adjoint(2)
    y_gather.finish()
    heads[1].second()
    weights.first()
    heads[1].last()
    inside_grad(0)
    inside_grad(2)
    weights.second()
    heads[1].finish()
    local_adjoint(1)
    local_adjoint(3)

    ADJ[0] = PART[SPANS - 1]
    for s in reversed(range(SPANS - 1)):
        ADJ[0] = jnp.exp(CUME[pl.ds(Q * s + Q - 1, 1), :]) * ADJ[0] + PART[s]
    ST[1] = ADJ[0].astype(BF)
    backward = Exchange(ST.at[1], AL, AB, AE, bex_sem, ci, hi)
    backward.start()
    inside_grad(1)
    inside_grad(3)
    c_sum = HeadSum(CP, CL, CT, CW, c_sem, ci, hi)
    c_sum.start()
    backward.landed()
    backward.scan(DEC, reversed(range(N_CTX)))
    backward.reply()
    weights.last()
    c_sum.reduce()
    backward.replied()
    ADJ[SPANS] = AE[...].astype(F32)
    for s in reversed(range(SPANS)):
        rows = pl.ds(Q * s, Q)
        BP[rows, :] = (B0[rows, :] + dot(XT[rows, :], ADJ[s + 1].astype(BF), NT)).astype(BF)
        if s > 0:
            ADJ[s] = jnp.exp(CUME[pl.ds(Q * s + Q - 1, 1), :]) * ADJ[s + 1] + PART[s]
    b_sum = HeadSum(BP, BL, BT, BW, b_sem, ci, hi)
    b_sum.start()

    def closing(s):
        rows = aligned(Q * s, Q, Q)
        cume = CUME[rows, :]
        total = cume[Q - 1 : Q, :]
        adjoint = ADJ[s + 1]
        in_grad = IG[rows, :] + jnp.exp(total - cume) * dot(b[rows, :], adjoint.astype(BF))
        IGB[rows, :] = in_grad.astype(BF)
        gk = GK[rows, :].astype(F32)
        step = XS[rows, :].astype(F32) * in_grad - gk * YF[rows, :]
        start = jnp.sum(gk * YI[rows, :], axis=0, keepdims=True) + jnp.exp(total) * jnp.sum(
            adjoint * STIN[s], axis=0, keepdims=True
        )
        row = lax.broadcasted_iota(jnp.int32, (Q, COLS), 0)
        step = jnp.where(row == 0, start, pltpu.roll(step, 1, 0))
        high = step.astype(BF)
        rest = (step - high.astype(F32)).astype(BF)
        steps = dot(E16B[...], high, NT) + dot(E16B[...], rest, NT)
        O_D[:, rows] = dot(steps, upto, precision=HIGH) * (1.0 / math.sqrt(P_SIZE * D))

    def spread_in(i):
        rows = aligned(128 * i, 128, 128)
        O_IG[rows, :] = dot(IGB[rows, :], S[...], NT).astype(BF)

    def spread_w(i):
        cols = aligned(128 * i, 128, 128)
        block = (weights.result(slice(None), cols) * (1.0 / math.sqrt(D))).astype(BF)
        O_W[cols, :] = dot(block, S[...], (((0,), (1,)), ((), ()))).astype(BF)

    stores = [
        pltpu.make_async_copy(src, dst, out_sem.at[i])
        for i, (src, dst) in enumerate(((O_IG, out_ig), (O_B, out_b), (O_C, out_c), (O_D, out_decay), (O_W, out_w)))
    ]
    loop(0, SPANS, closing)
    stores[3].start()
    b_sum.reduce()
    loop(0, TOK // 128, spread_in)
    stores[0].start()
    weights.finish()
    loop(0, TOK // 128, spread_w)
    stores[4].start()
    c_sum.finish()
    O_C[...] = CW[...].astype(F32) * math.sqrt(N / (KEPT * P_SIZE * D))
    stores[2].start()
    b_sum.finish()
    O_B[...] = BW[...].astype(F32) / math.sqrt(KEPT * P_SIZE)
    stores[1].start()

    for q in range(2):
        for p in range(2):

            @pl.when(2 * cc + p != y)
            def _():
                a2a_copy(q, p, 0).wait_send()

        for t in range(2):
            x_gathers[q][t].drain()
            for j in range(4):
                sibling_copy(q, t, j, cc).wait_send()
        heads[q].drain()
    w_gather.drain()
    y_gather.drain()
    weights.drain()
    loop(1, N_CTX, lambda k: decay_copy(k, ci).wait_send())
    forward.drain()
    backward.drain()
    c_sum.drain()
    b_sum.drain()
    for store in stores:
        store.wait()


def hand_over(*refs):
    count = len(refs) // 3
    ins, outs, held, sems = refs[:count], refs[count : 2 * count], refs[2 * count : -1], refs[-1]
    reads = [pltpu.make_async_copy(ins[i], held[i], sems.at[0, i]) for i in range(count)]
    writes = [pltpu.make_async_copy(held[i], outs[i], sems.at[1, i]) for i in range(count)]
    for read in reads:
        read.start()
    for read, write in zip(reads, writes):
        read.wait()
        write.start()
    for write in writes:
        write.wait()


def per_device(g_out, w_out, x_act, b_proj, c_proj, log_decay, kept_heads):
    hbm = pl.BlockSpec(memory_space=pl.ANY)
    buf = pltpu.VMEM
    dma = pltpu.SemaphoreType.DMA

    def ring(rows, cols):
        h = rows // 2
        return [
            buf((rows, cols), BF), buf((rows, cols), BF), buf((rows, cols), BF), buf((h, cols), BF), buf((h, cols), BF),
            buf((rows, cols), BF), buf((rows, cols), BF), buf((rows, cols), F32),
        ]

    def head_sum():
        return [
            buf((TOK, N), BF), buf((N_HEAD, TOK // N_HEAD, N), BF), buf((TOK // N_HEAD, N), BF), buf((TOK, N), BF)
        ]

    outs = (
        jax.ShapeDtypeStruct((TOK, WIDE), BF),
        jax.ShapeDtypeStruct((TOK, N), F32),
        jax.ShapeDtypeStruct((TOK, N), F32),
        jax.ShapeDtypeStruct((GROUP, TOK), F32),
        jax.ShapeDtypeStruct((TOK, WIDE), BF),
    )
    results = pl.pallas_call(
        kernel,
        out_shape=outs,
        in_specs=[pl.BlockSpec(memory_space=pltpu.SMEM)] + [hbm] * 6,
        out_specs=[hbm] * 5,
        scratch_shapes=[
            buf((TOK, WIDE), BF), buf((TOK, WIDE), BF), buf((TOK, N), BF), buf((TOK, N), BF), buf((GROUP, TOK), F32),
            buf((WIDE, COLS), BF), buf((GROUP, COLS), F32), buf((GROUP, COLS), BF),
            buf((4, 2, 2, TOK // 4, 4 * TOK), BF), buf((4 * TOK, COLS), BF), buf((COLS, 4 * TOK), BF),
            buf((TOK, COLS), BF), buf((TOK, COLS), BF), buf((TOK, COLS), F32), buf((GROUP, TOK), F32),
            buf((SPANS, N, COLS), F32), buf((SPANS + 1, N, COLS), F32), buf((SPANS + 1, N, COLS), F32),
            buf((TOK, COLS), F32), buf((TOK, COLS), F32),
            buf((SPANS * PAIRS, 2 * Q, Q), F32), buf((SPANS * PAIRS, 2 * Q, Q), BF),
            buf((TOK, COLS), BF), buf((TOK, COLS), BF), buf((TOK, COLS), F32), buf((TOK, COLS), BF),
            buf((TOK, N), F32),
            buf((8, 128), F32), buf((8 * N_CTX, 128), F32), buf((8 * N_CTX, HALF), F32), buf((2, N, COLS), BF),
            buf((16 * N_CTX, HALF), BF), buf((16 * N_CTX, HALF), BF), buf((N, COLS), BF),
            buf((16 * N_CTX, HALF), BF), buf((16 * N_CTX, HALF), BF), buf((N, COLS), BF),
            *head_sum(), *head_sum(),
            buf((TOK, WIDE), BF), buf((TOK, N), F32), buf((TOK, N), F32), buf((GROUP, TOK), F32), buf((TOK, WIDE), BF),
            *ring(TOK // 2, COLS), *ring(TOK // 2, COLS), *ring(COLS, TOK),
            dma((5,)), dma((2,)), dma((2, 2, 2)), dma((2, 2, 4)), dma((2, 2, 4)), dma((2, 2, 2, 4)), dma((2, 4)),
            dma((2, 4)), dma((2, 2, 6)), dma((2, 6)), dma((2, N_CTX)), dma((4, N_CTX)), dma((4, N_CTX)),
            dma((4, N_HEAD)), dma((4, N_HEAD)), dma((5,)),
        ],
        compiler_params=pltpu.CompilerParams(
            collective_id=0, has_side_effects=True, vmem_limit_bytes=VMEM_LIMIT
        ),
        cost_estimate=pl.CostEstimate(flops=14_000_000_000, bytes_accessed=8_000_000, transcendentals=4_000_000),
    )(
        kept_heads, g_out.reshape(2, 2, TOK // 4, WIDE), w_out, x_act, b_proj, c_proj, log_decay,
    )
    return pl.pallas_call(
        hand_over,
        out_shape=outs,
        in_specs=[hbm] * 5,
        out_specs=[hbm] * 5,
        scratch_shapes=[*(buf(out.shape, out.dtype) for out in outs), dma((2, 5))],
        compiler_params=pltpu.CompilerParams(has_side_effects=True, vmem_limit_bytes=VMEM_LIMIT),
    )(*results)


def solution(mesh):
    in_specs = (
        P("ctx", "head"),
        P("ctx", "head"),
        P("ctx", "head"),
        P("ctx", None),
        P("ctx", None),
        P("head", "ctx"),
        P(),
    )
    out_specs = (
        P("ctx", "head"),
        P("ctx", None),
        P("ctx", None),
        P("head", "ctx"),
        P("ctx", "head"),
    )
    return jax.shard_map(
        per_device, mesh=mesh, in_specs=in_specs, out_specs=out_specs, check_vma=False
    )
```

time: 162 us -> 136 us (0.84)
  Pallas kernels: 153 us -> 135 us
  local copies, waits for them, and re-layouts: 7.43 us -> 0 us
    pallas_call x1 -> x2, Pallas kernels: 153 us -> 135 us  [the longest x1 133 us: per_device(): pl.pallas_call(kernel, out_shape=outs, in_specs=[pl.BlockSpec(memory_spac...]
    unnamed x15 -> x0, local copies, waits for them, and re-layouts: 5.97 us -> none
where the time goes in v2:
time: 136 us
  Pallas kernels  135 us (99%)
    pallas_call x1, Pallas kernels, per_device(): pl.pallas_call(kernel, out_shape=outs, in_specs=[pl.BlockSpec(memory_spac...  133 us
    pallas_call x1, Pallas kernels, per_device(): pl.pallas_call(hand_over, out_shape=outs, in_specs=[hbm] * 5, out_specs=[...  2.81 us

profile of v2, /device:TPU:1, one launch (start us, length us, event | category | flops | bytes accessed | tf_op | source)
XLA Modules:
  0.0 136.2 jit_solution(4056320551767303814)
XLA Ops:
  0.6 132.6 %shard_map.110 = (bf16[512,1024]{1,0:T(8,128)(2,1)}, f32[512,128]{1,0:T(8,128)}, f32[512,128]{1,0:T(8,128)}, f32[16,512]{1,0:T(8,128)}, bf16[512,1024]{1,0:T(8,128)(2,1)}) custom-call(s32[64]{0:T(128)} %kept.1, bf16[2,2,128,1024]{3,2,1,0:T(8,128)(2,1)} %bitcast.1, bf16[512,1024]{1,0:T(8,128)(2,1)} %w_in.1, bf16[512,1024]{1,0:T(8,128)(2,1)} %x_in.1, ...), custom_call_target="tpu_custom_call" | custom-call | flops 14000000000 | bytes 8000000 | tf_op jit(solution)/shard_map/pallas_call | solution.py:720
  133.2 2.8 %shard_map.111 = (bf16[512,1024]{1,0:T(8,128)(2,1)}, f32[512,128]{1,0:T(8,128)}, f32[512,128]{1,0:T(8,128)}, f32[16,512]{1,0:T(8,128)}, bf16[512,1024]{1,0:T(8,128)(2,1)}) custom-call(bf16[512,1024]{1,0:T(8,128)(2,1)} %get-tuple-element.10.refs_0_, f32[512,128]{1,0:T(8,128)} %get-tuple-element.11.refs_1_, f32[512,128]{1,0:T(8,128)} %get-tuple-element.12.refs_2_, ...), custom_call_target="tpu_custom_call" | custom-call | tf_op jit(solution)/shard_map/pallas_call | solution.py:752

commit v3 on v2

--- a/solution.py
+++ b/solution.py
@@ -261,6 +261,13 @@
     r = lax.broadcasted_iota(jnp.int32, (rows, cols), 0)
     k = lax.broadcasted_iota(jnp.int32, (rows, cols), 1)
     return jnp.where(hit(r, k), 1.0, 0.0).astype(F32)
+
+
+def parts(a):
+    high = a.astype(BF)
+    rest = a - high.astype(F32)
+    middle = rest.astype(BF)
+    return jnp.concatenate([high, middle, (rest - middle.astype(F32)).astype(BF)], axis=0)
 
 
 def kernel(
@@ -325,83 +332,28 @@
 
     loop(0, WIDE // 128, build)
     E16[...] = jnp.where(lax.broadcasted_iota(jnp.int32, (GROUP, COLS), 0) == headof, 1.0, 0.0).astype(F32)
-    E16B[...] = E16[...].astype(BF)
-
-    pl.semaphore_wait(barrier, N_CTX - 1 + N_HEAD - 1 + 2 * cross)
-
-    def g_tile(token, feature, q):
-        return G.at[token, :, q, :, aligned(TOK * feature, TOK, TOK)]
-
-    def quarter(q, p):
-        return g.at[:, q, :, pl.ds(TOK * p, TOK)]
-
-    def a2a_copy(q, p, slot):
-        return rcopy(
-            quarter(q, p), g_tile(y, xx, q), a2a_sem.at[0, q, p], a2a_sem.at[1, q, slot], (4 * z + 2 * cc + p, 2 * xx + half)
-        )
-
-    def a2a_start(q):
-        for p in range(2):
-
-            @pl.when(2 * cc + p == y)
-            def _():
-                pltpu.make_async_copy(quarter(q, p), g_tile(y, xx, q), own_sem.at[q]).start()
-
-            @pl.when(2 * cc + p != y)
-            def _():
-                a2a_copy(q, p, lax.rem(y, 2)).start()
-
-    def a2a_landed(q, t):
-        token = 2 * cc + t
-
-        @pl.when(token == y)
-        def _():
-            pltpu.make_async_copy(quarter(q, 0), g_tile(token, xx, q), own_sem.at[q]).wait()
-
-        @pl.when(token != y)
-        def _():
-            rcopy(
-                quarter(q, 0), g_tile(token, xx, q), a2a_sem.at[0, q, t], a2a_sem.at[1, q, t], sibling
-            ).wait_recv()
-
-    a2a_start(0)
+    for i in range(3):
+        E16B[pl.ds(GROUP * i, GROUP), :] = E16[...].astype(BF)
 
     for load in loads:
         load.wait()
 
-    def pick_w(i):
-        W[aligned(TOK * z + 128 * i, 128, 128), :] = dot(w[aligned(128 * i, 128, 128), :], S[...]).astype(BF)
-
-    loop(0, TOK // 128, pick_w)
-    w_gather = Gather(
-        lambda p: W.at[aligned(TOK * p, TOK, TOK), :],
-        lambda p, h: W.at[aligned(TOK * p + TOK // 2 * h, TOK // 2, TOK // 2), :],
-        lambda i: wag_sem.at[0, i],
-        lambda i: wag_sem.at[1, i],
-        z, prv(z), nxt(z), at_z,
-    )
-    w_gather.start()
-
     upto = one_hot(Q, Q, lambda r, k: r <= k)
     pick = one_hot(COLS, 128, lambda r, k: r == P_SIZE * k)
-    slots = dot(E16[...], pick)[:, :GROUP]
+    slots = dot(E16[...], pick)[:, :GROUP].astype(BF)
+    slots3 = jnp.concatenate([slots] * 3, axis=0)
+    upto_low = upto.astype(BF)
 
     def decays(s):
         rows = aligned(Q * s, Q, Q)
-        cum = dot(logd[:, rows], upto, precision=HIGH)
-        CUMR[:, rows] = dot(slots, cum, TN, precision=HIGH)
-        CUME[rows, :] = dot(cum, E16[...], TN, precision=HIGH)
+        sums = dot(parts(logd[:, rows]), upto_low)
+        cum = parts(sums[:GROUP] + sums[GROUP : 2 * GROUP] + sums[2 * GROUP :])
+        CUMR[:, rows] = dot(slots3, cum, TN)
+        CUME[rows, :] = dot(cum, E16B[...], TN)
 
     loop(0, SPANS, decays)
     totals = sum(CUMR[:, pl.ds(Q * s + Q - 1, 1)] for s in range(SPANS))
     TOT[...] = dot(jnp.broadcast_to(totals, (GROUP, 8)), one_hot(GROUP, 128, lambda r, k: r == k), TN, precision=HIGH)
-
-    def decay_copy(k, at):
-        to = lax.rem(ci + k, N_CTX)
-        return rcopy(TOT, RD.at[aligned(8 * at, 8, 8), :], dec_sem.at[0, k], dec_sem.at[1, k], (to, hi))
-
-    loop(1, N_CTX, lambda k: decay_copy(k, ci).start())
-    RD[aligned(8 * ci, 8, 8), :] = TOT[...]
 
     STIN[0] = jnp.zeros((N, COLS), F32)
 
@@ -419,8 +371,37 @@
 
     loop(0, SPANS, local_states)
     ST[0] = STIN[0].astype(BF)
+
+    pl.semaphore_wait(barrier, N_CTX - 1 + N_HEAD - 1 + 2 * cross)
+
+    def decay_copy(k, at):
+        to = lax.rem(ci + k, N_CTX)
+        return rcopy(TOT, RD.at[aligned(8 * at, 8, 8), :], dec_sem.at[0, k], dec_sem.at[1, k], (to, hi))
+
+    loop(1, N_CTX, lambda k: decay_copy(k, ci).start())
+    RD[aligned(8 * ci, 8, 8), :] = TOT[...]
+
     forward = Exchange(ST.at[0], FL, FB, FE, fex_sem, ci, hi)
     forward.start()
+
+
+    def g_tile(token, feature, q):
+        return G.at[token, :, q, :, aligned(TOK * feature, TOK, TOK)]
+
+    def quarter(q, p):
+        return g.at[:, q, :, pl.ds(TOK * p, TOK)]
+
+    def a2a_copy(q, p, slot):
+        return rcopy(
+            quarter(q, p), g_tile(y, xx, q), a2a_sem.at[0, q, p], a2a_sem.at[1, q, slot], (4 * z + 2 * cc + p, 2 * xx + half)
+        )
+
+    def a2a_start(q):
+        for p in range(2):
+
+            @pl.when(2 * cc + p != y)
+            def _():
+                a2a_copy(q, p, lax.rem(y, 2)).start()
 
     def x_gather(q, t):
         token = 2 * cc + t
@@ -439,11 +420,33 @@
         tile = g_tile(2 * core + t, ring_x[j], q)
         return rcopy(tile, tile, sib_sem.at[0, q, t, j], sib_sem.at[1, q, t, j], sibling)
 
-    def x_start(q):
+    def x_launch(q, t):
+        x_gathers[q][t].start()
+        sibling_copy(q, t, 0, cc).start()
+
+    def own_copy(q, p):
+        return pltpu.make_async_copy(quarter(q, p), g_tile(y, xx, q), own_sem.at[q])
+
+    def x_own():
+        for p in range(2):
+
+            @pl.when(2 * cc + p == y)
+            def _():
+                for q in range(2):
+                    own_copy(q, p).start()
+                for q in range(2):
+                    own_copy(q, p).wait()
+                    x_launch(q, p)
+
+    def x_rest(q):
         for t in range(2):
-            a2a_landed(q, t)
-            x_gathers[q][t].start()
-            sibling_copy(q, t, 0, cc).start()
+
+            @pl.when(2 * cc + t != y)
+            def _():
+                rcopy(
+                    quarter(q, t), g_tile(2 * cc + t, xx, q), a2a_sem.at[0, q, t], a2a_sem.at[1, q, t], sibling
+                ).wait_recv()
+                x_launch(q, t)
 
     def x_forward(q):
         for t in range(2):
@@ -459,9 +462,12 @@
             for j in range(4):
                 sibling_copy(q, t, j, 1 - cc).wait_recv()
 
-    x_start(0)
-    a2a_start(1)
-
+    x_own()
+
+    def pick_w(i):
+        W[aligned(TOK * z + 128 * i, 128, 128), :] = dot(w[aligned(128 * i, 128, 128), :], S[...]).astype(BF)
+
+    loop(0, TOK // 128, pick_w)
     sub = lax.broadcasted_iota(jnp.int32, (Q, Q), 0)
     lane = lax.broadcasted_iota(jnp.int32, (Q, Q), 1)
     left_half = lane < P_SIZE
@@ -489,7 +495,15 @@
     forward.landed()
     forward.scan(DEC, range(N_CTX))
     forward.reply()
-    w_gather.forward()
+    a2a_start(0)
+    w_gather = Gather(
+        lambda p: W.at[aligned(TOK * p, TOK, TOK), :],
+        lambda p, h: W.at[aligned(TOK * p + TOK // 2 * h, TOK // 2, TOK // 2), :],
+        lambda i: wag_sem.at[0, i],
+        lambda i: wag_sem.at[1, i],
+        z, prv(z), nxt(z), at_z,
+    )
+    w_gather.start()
     forward.replied()
     STIN[0] = FE[...].astype(F32)
 
@@ -558,27 +572,29 @@
         B0[rows, :] = dot(sg, c[rows, :], TN)
         CP[rows, :] = (dot(sg, b[rows, :]) + dot(GH[rows, :], STIN[s].astype(BF), NT)).astype(BF)
 
+    x_rest(0)
+    a2a_start(1)
+    w_gather.forward()
     x_forward(0)
-    x_start(1)
+    x_rest(1)
+    y_gather.forward()
     w_gather.finish()
     x_finish(0)
     heads[0].first()
     x_forward(1)
-    y_gather.forward()
+    x_finish(1)
     heads[0].second()
+    y_gather.finish()
+    weights.first()
+    heads[1].first()
     heads[0].last()
-    x_finish(1)
-    heads[1].first()
     heads[0].finish()
     local_adjoint(0)
     local_adjoint(2)
-    y_gather.finish()
     heads[1].second()
-    weights.first()
     heads[1].last()
     inside_grad(0)
     inside_grad(2)
-    weights.second()
     heads[1].finish()
     local_adjoint(1)
     local_adjoint(3)
@@ -596,6 +612,7 @@
     backward.landed()
     backward.scan(DEC, reversed(range(N_CTX)))
     backward.reply()
+    weights.second()
     weights.last()
     c_sum.reduce()
     backward.replied()
@@ -624,7 +641,7 @@
         step = jnp.where(row == 0, start, pltpu.roll(step, 1, 0))
         high = step.astype(BF)
         rest = (step - high.astype(F32)).astype(BF)
-        steps = dot(E16B[...], high, NT) + dot(E16B[...], rest, NT)
+        steps = dot(E16B[:GROUP], high, NT) + dot(E16B[:GROUP], rest, NT)
         O_D[:, rows] = dot(steps, upto, precision=HIGH) * (1.0 / math.sqrt(P_SIZE * D))
 
     def spread_in(i):
@@ -724,7 +741,7 @@
         out_specs=[hbm] * 5,
         scratch_shapes=[
             buf((TOK, WIDE), BF), buf((TOK, WIDE), BF), buf((TOK, N), BF), buf((TOK, N), BF), buf((GROUP, TOK), F32),
-            buf((WIDE, COLS), BF), buf((GROUP, COLS), F32), buf((GROUP, COLS), BF),
+            buf((WIDE, COLS), BF), buf((GROUP, COLS), F32), buf((3 * GROUP, COLS), BF),
             buf((4, 2, 2, TOK // 4, 4 * TOK), BF), buf((4 * TOK, COLS), BF), buf((COLS, 4 * TOK), BF),
             buf((TOK, COLS), BF), buf((TOK, COLS), BF), buf((TOK, COLS), F32), buf((GROUP, TOK), F32),
             buf((SPANS, N, COLS), F32), buf((SPANS + 1, N, COLS), F32), buf((SPANS + 1, N, COLS), F32),

time: 136 us -> 117 us (0.86)
  Pallas kernels: 135 us -> 116 us
    pallas_call x1, Pallas kernels: 133 us -> 114 us  [per_device(): pl.pallas_call(kernel, out_shape=outs, in_specs=[pl.BlockSpec(memory_spac...]
where the time goes in v3:
time: 117 us
  Pallas kernels  116 us (99%)
    pallas_call x1, Pallas kernels, per_device(): pl.pallas_call(kernel, out_shape=outs, in_specs=[pl.BlockSpec(memory_spac...  114 us
    pallas_call x1, Pallas kernels, per_device(): pl.pallas_call(hand_over, out_shape=outs, in_specs=[hbm] * 5, out_specs=[...  2.81 us

profile of v3, /device:TPU:1, one launch (start us, length us, event | category | flops | bytes accessed | tf_op | source)
XLA Modules:
  0.0 117.3 jit_solution(16035459152072563819)
XLA Ops:
  0.6 113.6 %shard_map.110 = (bf16[512,1024]{1,0:T(8,128)(2,1)}, f32[512,128]{1,0:T(8,128)}, f32[512,128]{1,0:T(8,128)}, f32[16,512]{1,0:T(8,128)}, bf16[512,1024]{1,0:T(8,128)(2,1)}) custom-call(s32[64]{0:T(128)} %kept.1, bf16[2,2,128,1024]{3,2,1,0:T(8,128)(2,1)} %bitcast.1, bf16[512,1024]{1,0:T(8,128)(2,1)} %w_in.1, bf16[512,1024]{1,0:T(8,128)(2,1)} %x_in.1, ...), custom_call_target="tpu_custom_call" | custom-call | flops 14000000000 | bytes 8000000 | tf_op jit(solution)/shard_map/pallas_call | solution.py:737
  114.3 2.8 %shard_map.111 = (bf16[512,1024]{1,0:T(8,128)(2,1)}, f32[512,128]{1,0:T(8,128)}, f32[512,128]{1,0:T(8,128)}, f32[16,512]{1,0:T(8,128)}, bf16[512,1024]{1,0:T(8,128)(2,1)}) custom-call(bf16[512,1024]{1,0:T(8,128)(2,1)} %get-tuple-element.10.refs_0_, f32[512,128]{1,0:T(8,128)} %get-tuple-element.11.refs_1_, f32[512,128]{1,0:T(8,128)} %get-tuple-element.12.refs_2_, ...), custom_call_target="tpu_custom_call" | custom-call | tf_op jit(solution)/shard_map/pallas_call | solution.py:769

commit v4 on v3

--- a/solution.py
+++ b/solution.py
@@ -213,9 +213,12 @@
 
 
 class HeadSum:
-    def __init__(self, part, landed, total, whole, sems, ci, hi):
+    def __init__(self, part, landed, total, whole, sems, own_sem, ci, hi):
         self.part, self.landed_ref, self.total, self.whole = part, landed, total, whole
-        self.sems, self.ci, self.hi = sems, ci, hi
+        self.sems, self.own_sem, self.ci, self.hi = sems, own_sem, ci, hi
+
+    def own_copy(self):
+        return pltpu.make_async_copy(self.total, self.whole.at[self.share(self.hi), :], self.own_sem)
 
     def share(self, r):
         return aligned(TOK // N_HEAD * r, TOK // N_HEAD, TOK // N_HEAD)
@@ -244,10 +247,11 @@
             total = total + self.landed_ref[i].astype(F32)
         self.total[...] = total.astype(BF)
         loop(1, N_HEAD, lambda k: self.back_copy(k, self.hi).start())
-        self.whole[self.share(self.hi), :] = self.total[...]
+        self.own_copy().start()
 
     def finish(self):
         loop(1, N_HEAD, lambda k: self.back_copy(k, lax.rem(self.hi + N_HEAD - k, N_HEAD)).wait_recv())
+        self.own_copy().wait()
 
     def drain(self):
         def one(k):
@@ -273,8 +277,8 @@
 def kernel(
     kept, g, w_in, x_in, b_in, c_in, logd_in,
     out_ig, out_b, out_c, out_decay, out_w,
-    w, x, b, c, logd, S, E16, E16B, G, W, YT, XS, XT, CUME, CUMR, PART, STIN, ADJ, YF, YI, L, MS, GK, GH, IG, IGB, B0,
-    TOT, RD, DEC, ST, FL, FB, FE, AL, AB, AE, BP, BL, BT, BW, CP, CL, CT, CW, O_IG, O_B, O_C, O_D, O_W,
+    w, x, b, c, logd, S, S_T, E16, E16B, G, W, YT, XS, XT, CUME, CUMR, PART, STIN, ADJ, YF, YI, L, MS, GK, GH, IG, IGB, B0,
+    AFTER, TOT, RD, DEC, ST, FL, FB, FE, AL, AB, AE, BP, BL, BT, CP, CL, CT, O_IG, O_D, O_W,
     a_far, a_right, a_left, a_vl, a_vr, a_fl, a_fr, a_own,
     b_far, b_right, b_left, b_vl, b_vr, b_fl, b_fr, b_own,
     w_far, w_right, w_left, w_vl, w_vr, w_fl, w_fr, w_own,
@@ -462,12 +466,24 @@
             for j in range(4):
                 sibling_copy(q, t, j, 1 - cc).wait_recv()
 
+    a2a_start(0)
     x_own()
 
     def pick_w(i):
         W[aligned(TOK * z + 128 * i, 128, 128), :] = dot(w[aligned(128 * i, 128, 128), :], S[...]).astype(BF)
 
     loop(0, TOK // 128, pick_w)
+
+    def w_gather(q):
+        return Gather(
+            lambda p: W.at[aligned(TOK * p + TOK // 2 * q, TOK // 2, TOK // 2), :],
+            lambda p, h: W.at[aligned(TOK * p + TOK // 2 * q + TOK // 4 * h, TOK // 4, TOK // 4), :],
+            lambda i: wag_sem.at[q, 0, i],
+            lambda i: wag_sem.at[q, 1, i],
+            z, prv(z), nxt(z), at_z,
+        )
+
+    w_gathers = [w_gather(q) for q in range(2)]
     sub = lax.broadcasted_iota(jnp.int32, (Q, Q), 0)
     lane = lax.broadcasted_iota(jnp.int32, (Q, Q), 1)
     left_half = lane < P_SIZE
@@ -487,6 +503,11 @@
             both = dot(MS[PAIRS * s + k], XS[rows, cols])
             YF[rows, cols] = jnp.where(left_half, both[:Q], both[Q:])
 
+    rowidx = jnp.broadcast_to(colidx, (8, COLS)).astype(F32).T[:, 0:1].astype(jnp.int32)
+    for i in range(COLS // 128):
+        ids = lax.broadcasted_iota(jnp.int32, (128, WIDE), 1)
+        S_T[pl.ds(128 * i, 128), :] = jnp.where(ids == rowidx[128 * i : 128 * i + 128], 1.0, 0.0).astype(BF)
+
     loop(0, SPANS, inside)
 
     loop(1, N_CTX, lambda k: decay_copy(k, lax.rem(ci + N_CTX - k, N_CTX)).wait_recv())
@@ -495,15 +516,10 @@
     forward.landed()
     forward.scan(DEC, range(N_CTX))
     forward.reply()
-    a2a_start(0)
-    w_gather = Gather(
-        lambda p: W.at[aligned(TOK * p, TOK, TOK), :],
-        lambda p, h: W.at[aligned(TOK * p + TOK // 2 * h, TOK // 2, TOK // 2), :],
-        lambda i: wag_sem.at[0, i],
-        lambda i: wag_sem.at[1, i],
-        z, prv(z), nxt(z), at_z,
-    )
-    w_gather.start()
+    w_gathers[0].start()
+    w_gathers[1].start()
+    a2a_start(1)
+    x_rest(0)
     forward.replied()
     STIN[0] = FE[...].astype(F32)
 
@@ -572,16 +588,16 @@
         B0[rows, :] = dot(sg, c[rows, :], TN)
         CP[rows, :] = (dot(sg, b[rows, :]) + dot(GH[rows, :], STIN[s].astype(BF), NT)).astype(BF)
 
-    x_rest(0)
-    a2a_start(1)
-    w_gather.forward()
     x_forward(0)
     x_rest(1)
+    w_gathers[0].forward()
+    w_gathers[1].forward()
     y_gather.forward()
-    w_gather.finish()
+    x_forward(1)
+    w_gathers[0].finish()
+    w_gathers[1].finish()
     x_finish(0)
     heads[0].first()
-    x_forward(1)
     x_finish(1)
     heads[0].second()
     y_gather.finish()
@@ -599,16 +615,44 @@
     local_adjoint(1)
     local_adjoint(3)
 
-    ADJ[0] = PART[SPANS - 1]
-    for s in reversed(range(SPANS - 1)):
-        ADJ[0] = jnp.exp(CUME[pl.ds(Q * s + Q - 1, 1), :]) * ADJ[0] + PART[s]
+    ADJ[SPANS] = jnp.zeros((N, COLS), F32)
+    after = jnp.zeros((1, COLS), F32)
+    for s in reversed(range(SPANS)):
+        total = CUME[pl.ds(Q * s + Q - 1, 1), :]
+        AFTER[pl.ds(s, 1), :] = jnp.exp(after)
+        after = after + total
+        ADJ[s] = jnp.exp(total) * ADJ[s + 1] + PART[s]
     ST[1] = ADJ[0].astype(BF)
     backward = Exchange(ST.at[1], AL, AB, AE, bex_sem, ci, hi)
     backward.start()
     inside_grad(1)
     inside_grad(3)
-    c_sum = HeadSum(CP, CL, CT, CW, c_sem, ci, hi)
+
+    def local_b(s):
+        rows = aligned(Q * s, Q, Q)
+        B0[rows, :] = B0[rows, :] + dot(XT[rows, :], ADJ[s + 1].astype(BF), NT)
+
+    loop(0, SPANS - 1, local_b)
+    c_sum = HeadSum(CP, CL, CT, out_c, c_sem, out_sem.at[1], ci, hi)
     c_sum.start()
+
+    loop(1, N_CTX, lambda k: decay_copy(k, ci).wait_send())
+    forward.drain()
+    for q in range(2):
+        w_gathers[q].drain()
+    y_gather.drain()
+    for q in range(2):
+        for p in range(2):
+
+            @pl.when(2 * cc + p != y)
+            def _():
+                a2a_copy(q, p, 0).wait_send()
+
+        for t in range(2):
+            x_gathers[q][t].drain()
+            for j in range(4):
+                sibling_copy(q, t, j, cc).wait_send()
+
     backward.landed()
     backward.scan(DEC, reversed(range(N_CTX)))
     backward.reply()
@@ -616,20 +660,21 @@
     weights.last()
     c_sum.reduce()
     backward.replied()
-    ADJ[SPANS] = AE[...].astype(F32)
-    for s in reversed(range(SPANS)):
-        rows = pl.ds(Q * s, Q)
-        BP[rows, :] = (B0[rows, :] + dot(XT[rows, :], ADJ[s + 1].astype(BF), NT)).astype(BF)
-        if s > 0:
-            ADJ[s] = jnp.exp(CUME[pl.ds(Q * s + Q - 1, 1), :]) * ADJ[s + 1] + PART[s]
-    b_sum = HeadSum(BP, BL, BT, BW, b_sem, ci, hi)
+
+    def whole_b(s):
+        rows = aligned(Q * s, Q, Q)
+        carried = (AFTER[pl.ds(s, 1), :] * AE[...].astype(F32)).astype(BF)
+        BP[rows, :] = (B0[rows, :] + dot(XT[rows, :], carried, NT)).astype(BF)
+
+    loop(0, SPANS, whole_b)
+    b_sum = HeadSum(BP, BL, BT, out_b, b_sem, out_sem.at[2], ci, hi)
     b_sum.start()
 
     def closing(s):
         rows = aligned(Q * s, Q, Q)
         cume = CUME[rows, :]
         total = cume[Q - 1 : Q, :]
-        adjoint = ADJ[s + 1]
+        adjoint = ADJ[s + 1] + AFTER[pl.ds(s, 1), :] * AE[...].astype(F32)
         in_grad = IG[rows, :] + jnp.exp(total - cume) * dot(b[rows, :], adjoint.astype(BF))
         IGB[rows, :] = in_grad.astype(BF)
         gk = GK[rows, :].astype(F32)
@@ -646,66 +691,53 @@
 
     def spread_in(i):
         rows = aligned(128 * i, 128, 128)
-        O_IG[rows, :] = dot(IGB[rows, :], S[...], NT).astype(BF)
+        O_IG[rows, :] = dot(IGB[rows, :], S_T[...]).astype(BF)
 
     def spread_w(i):
         cols = aligned(128 * i, 128, 128)
         block = (weights.result(slice(None), cols) * (1.0 / math.sqrt(D))).astype(BF)
-        O_W[cols, :] = dot(block, S[...], (((0,), (1,)), ((), ()))).astype(BF)
+        O_W[cols, :] = dot(block, S_T[...], TN).astype(BF)
 
     stores = [
-        pltpu.make_async_copy(src, dst, out_sem.at[i])
-        for i, (src, dst) in enumerate(((O_IG, out_ig), (O_B, out_b), (O_C, out_c), (O_D, out_decay), (O_W, out_w)))
+        pltpu.make_async_copy(O_IG, out_ig, out_sem.at[0]),
+        pltpu.make_async_copy(O_D, out_decay, out_sem.at[3]),
+        pltpu.make_async_copy(O_W, out_w, out_sem.at[4]),
     ]
     loop(0, SPANS, closing)
-    stores[3].start()
+    stores[1].start()
     b_sum.reduce()
     loop(0, TOK // 128, spread_in)
     stores[0].start()
     weights.finish()
     loop(0, TOK // 128, spread_w)
-    stores[4].start()
+    stores[2].start()
     c_sum.finish()
-    O_C[...] = CW[...].astype(F32) * math.sqrt(N / (KEPT * P_SIZE * D))
-    stores[2].start()
-    b_sum.finish()
-    O_B[...] = BW[...].astype(F32) / math.sqrt(KEPT * P_SIZE)
-    stores[1].start()
-
-    for q in range(2):
-        for p in range(2):
-
-            @pl.when(2 * cc + p != y)
-            def _():
-                a2a_copy(q, p, 0).wait_send()
-
-        for t in range(2):
-            x_gathers[q][t].drain()
-            for j in range(4):
-                sibling_copy(q, t, j, cc).wait_send()
-        heads[q].drain()
-    w_gather.drain()
-    y_gather.drain()
+    heads[0].drain()
+    heads[1].drain()
     weights.drain()
-    loop(1, N_CTX, lambda k: decay_copy(k, ci).wait_send())
-    forward.drain()
     backward.drain()
     c_sum.drain()
+    b_sum.finish()
+
     b_sum.drain()
     for store in stores:
         store.wait()
 
 
 def hand_over(*refs):
-    count = len(refs) // 3
-    ins, outs, held, sems = refs[:count], refs[count : 2 * count], refs[2 * count : -1], refs[-1]
-    reads = [pltpu.make_async_copy(ins[i], held[i], sems.at[0, i]) for i in range(count)]
-    writes = [pltpu.make_async_copy(held[i], outs[i], sems.at[1, i]) for i in range(count)]
+    ins, outs, held, scaled, sems = refs[:5], refs[5:10], refs[10:15], refs[15:17], refs[17]
+    sources = [held[0], *scaled, held[3], held[4]]
+    reads = [pltpu.make_async_copy(ins[i], held[i], sems.at[0, i]) for i in range(5)]
+    writes = [pltpu.make_async_copy(sources[i], outs[i], sems.at[1, i]) for i in range(5)]
     for read in reads:
         read.start()
-    for read, write in zip(reads, writes):
-        read.wait()
-        write.start()
+    for i in (0, 4, 3, 1, 2):
+        reads[i].wait()
+        if i == 1:
+            scaled[0][...] = held[1][...].astype(F32) / math.sqrt(KEPT * P_SIZE)
+        if i == 2:
+            scaled[1][...] = held[2][...].astype(F32) * math.sqrt(N / (KEPT * P_SIZE * D))
+        writes[i].start()
     for write in writes:
         write.wait()
 
@@ -724,7 +756,7 @@
 
     def head_sum():
         return [
-            buf((TOK, N), BF), buf((N_HEAD, TOK // N_HEAD, N), BF), buf((TOK // N_HEAD, N), BF), buf((TOK, N), BF)
+            buf((TOK, N), BF), buf((N_HEAD, TOK // N_HEAD, N), BF), buf((TOK // N_HEAD, N), BF)
         ]
 
     outs = (
@@ -734,14 +766,16 @@
         jax.ShapeDtypeStruct((GROUP, TOK), F32),
         jax.ShapeDtypeStruct((TOK, WIDE), BF),
     )
+    sums = jax.ShapeDtypeStruct((TOK, N), BF)
+    held = (outs[0], sums, sums, *outs[3:])
     results = pl.pallas_call(
         kernel,
-        out_shape=outs,
+        out_shape=held,
         in_specs=[pl.BlockSpec(memory_space=pltpu.SMEM)] + [hbm] * 6,
         out_specs=[hbm] * 5,
         scratch_shapes=[
             buf((TOK, WIDE), BF), buf((TOK, WIDE), BF), buf((TOK, N), BF), buf((TOK, N), BF), buf((GROUP, TOK), F32),
-            buf((WIDE, COLS), BF), buf((GROUP, COLS), F32), buf((3 * GROUP, COLS), BF),
+            buf((WIDE, COLS), BF), buf((COLS, WIDE), BF), buf((GROUP, COLS), F32), buf((3 * GROUP, COLS), BF),
             buf((4, 2, 2, TOK // 4, 4 * TOK), BF), buf((4 * TOK, COLS), BF), buf((COLS, 4 * TOK), BF),
             buf((TOK, COLS), BF), buf((TOK, COLS), BF), buf((TOK, COLS), F32), buf((GROUP, TOK), F32),
             buf((SPANS, N, COLS), F32), buf((SPANS + 1, N, COLS), F32), buf((SPANS + 1, N, COLS), F32),
@@ -749,13 +783,13 @@
             buf((SPANS * PAIRS, 2 * Q, Q), F32), buf((SPANS * PAIRS, 2 * Q, Q), BF),
             buf((TOK, COLS), BF), buf((TOK, COLS), BF), buf((TOK, COLS), F32), buf((TOK, COLS), BF),
             buf((TOK, N), F32),
-            buf((8, 128), F32), buf((8 * N_CTX, 128), F32), buf((8 * N_CTX, HALF), F32), buf((2, N, COLS), BF),
+            buf((8, COLS), F32), buf((8, 128), F32), buf((8 * N_CTX, 128), F32), buf((8 * N_CTX, HALF), F32), buf((2, N, COLS), BF),
             buf((16 * N_CTX, HALF), BF), buf((16 * N_CTX, HALF), BF), buf((N, COLS), BF),
             buf((16 * N_CTX, HALF), BF), buf((16 * N_CTX, HALF), BF), buf((N, COLS), BF),
             *head_sum(), *head_sum(),
-            buf((TOK, WIDE), BF), buf((TOK, N), F32), buf((TOK, N), F32), buf((GROUP, TOK), F32), buf((TOK, WIDE), BF),
+            buf((TOK, WIDE), BF), buf((GROUP, TOK), F32), buf((TOK, WIDE), BF),
             *ring(TOK // 2, COLS), *ring(TOK // 2, COLS), *ring(COLS, TOK),
-            dma((5,)), dma((2,)), dma((2, 2, 2)), dma((2, 2, 4)), dma((2, 2, 4)), dma((2, 2, 2, 4)), dma((2, 4)),
+            dma((5,)), dma((2,)), dma((2, 2, 2)), dma((2, 2, 4)), dma((2, 2, 4)), dma((2, 2, 2, 4)), dma((2, 2, 4)),
             dma((2, 4)), dma((2, 2, 6)), dma((2, 6)), dma((2, N_CTX)), dma((4, N_CTX)), dma((4, N_CTX)),
             dma((4, N_HEAD)), dma((4, N_HEAD)), dma((5,)),
         ],
@@ -771,7 +805,7 @@
         out_shape=outs,
         in_specs=[hbm] * 5,
         out_specs=[hbm] * 5,
-        scratch_shapes=[*(buf(out.shape, out.dtype) for out in outs), dma((2, 5))],
+        scratch_shapes=[*(buf(out.shape, out.dtype) for out in (*held, *outs[1:3])), dma((2, 5))],
         compiler_params=pltpu.CompilerParams(has_side_effects=True, vmem_limit_bytes=VMEM_LIMIT),
     )(*results)
 

time: 117 us -> 112 us (0.957)
  Pallas kernels: 116 us -> 111 us
    pallas_call x1, Pallas kernels: 114 us -> 108 us  [per_device(): pl.pallas_call(kernel, out_shape=held, in_specs=[pl.BlockSpec(memory_spac...]
where the time goes in v4:
time: 112 us
  Pallas kernels  111 us (99%)
    pallas_call x1, Pallas kernels, per_device(): pl.pallas_call(kernel, out_shape=held, in_specs=[pl.BlockSpec(memory_spac...  108 us
    pallas_call x1, Pallas kernels, per_device(): pl.pallas_call(hand_over, out_shape=outs, in_specs=[hbm] * 5, out_specs=[...  2.87 us

profile of v4, /device:TPU:1, one launch (start us, length us, event | category | flops | bytes accessed | tf_op | source)
XLA Modules:
  0.0 111.8 jit_solution(7360491949801502064)
XLA Ops:
  0.6 108.2 %shard_map.110 = (bf16[512,1024]{1,0:T(8,128)(2,1)}, bf16[512,128]{1,0:T(8,128)(2,1)}, bf16[512,128]{1,0:T(8,128)(2,1)}, f32[16,512]{1,0:T(8,128)}, bf16[512,1024]{1,0:T(8,128)(2,1)}) custom-call(s32[64]{0:T(128)} %kept.1, bf16[2,2,128,1024]{3,2,1,0:T(8,128)(2,1)} %bitcast.1, bf16[512,1024]{1,0:T(8,128)(2,1)} %w_in.1, bf16[512,1024]{1,0:T(8,128)(2,1)} %x_in.1, ...), custom_call_target="tpu_custom_call" | custom-call | flops 14000000000 | bytes 8000000 | tf_op jit(solution)/shard_map/pallas_call | solution.py:771
  108.8 2.9 %shard_map.111 = (bf16[512,1024]{1,0:T(8,128)(2,1)}, f32[512,128]{1,0:T(8,128)}, f32[512,128]{1,0:T(8,128)}, f32[16,512]{1,0:T(8,128)}, bf16[512,1024]{1,0:T(8,128)(2,1)}) custom-call(bf16[512,1024]{1,0:T(8,128)(2,1)} %get-tuple-element.10.refs_0_, bf16[512,128]{1,0:T(8,128)(2,1)} %get-tuple-element.11.refs_1_, bf16[512,128]{1,0:T(8,128)(2,1)} %get-tuple-element.12.refs_2_, ...), custom_call_target="tpu_custom_call" | custom-call | tf_op jit(solution)/shard_map/pallas_call | solution.py:803

commit v5 on v4

--- a/solution.py
+++ b/solution.py
@@ -534,15 +534,19 @@
         YT[:, aligned(TOK * y + Q * s, Q, Q)] = whole.T.astype(BF)
         STIN[s + 1] = jnp.exp(cume[Q - 1 : Q, :]) * state_in + PART[s]
 
-    loop(0, SPANS, outputs)
-    y_gather = Gather(
-        lambda p: YT.at[:, aligned(TOK * p, TOK, TOK)],
-        lambda p, h: YT.at[pl.ds(HALF * h, HALF), aligned(TOK * p, TOK, TOK)],
-        lambda i: yag_sem.at[0, i],
-        lambda i: yag_sem.at[1, i],
-        y, prv(y), nxt(y), at_y,
-    )
-    y_gather.start()
+    def y_gather(q):
+        return Gather(
+            lambda p: YT.at[:, aligned(TOK * p + TOK // 2 * q, TOK // 2, TOK // 2)],
+            lambda p, h: YT.at[pl.ds(HALF * h, HALF), aligned(TOK * p + TOK // 2 * q, TOK // 2, TOK // 2)],
+            lambda i: yag_sem.at[q, 0, i],
+            lambda i: yag_sem.at[q, 1, i],
+            y, prv(y), nxt(y), at_y,
+        )
+
+    y_gathers = [y_gather(q) for q in range(2)]
+    for q in range(2):
+        loop(SPANS // 2 * q, SPANS // 2 * (q + 1), outputs)
+        y_gathers[q].start()
 
     def head_term(q):
         return lambda block: dot(G[block, :, q].reshape(TOK // 2, 4 * TOK), W[...])
@@ -591,16 +595,18 @@
     x_forward(0)
     x_rest(1)
     w_gathers[0].forward()
+    y_gathers[0].forward()
     w_gathers[1].forward()
-    y_gather.forward()
     x_forward(1)
+    y_gathers[1].forward()
     w_gathers[0].finish()
     w_gathers[1].finish()
     x_finish(0)
     heads[0].first()
     x_finish(1)
     heads[0].second()
-    y_gather.finish()
+    y_gathers[0].finish()
+    y_gathers[1].finish()
     weights.first()
     heads[1].first()
     heads[0].last()
@@ -640,7 +646,8 @@
     forward.drain()
     for q in range(2):
         w_gathers[q].drain()
-    y_gather.drain()
+    y_gathers[0].drain()
+    y_gathers[1].drain()
     for q in range(2):
         for p in range(2):
 
@@ -727,17 +734,21 @@
 def hand_over(*refs):
     ins, outs, held, scaled, sems = refs[:5], refs[5:10], refs[10:15], refs[15:17], refs[17]
     sources = [held[0], *scaled, held[3], held[4]]
-    reads = [pltpu.make_async_copy(ins[i], held[i], sems.at[0, i]) for i in range(5)]
-    writes = [pltpu.make_async_copy(sources[i], outs[i], sems.at[1, i]) for i in range(5)]
+    cuts = [(i, pl.ds(TOK // 4 * k, TOK // 4)) for k in range(4) for i in (0, 4)]
+    cuts += [(3, pl.ds(0, GROUP)), (2, pl.ds(0, TOK)), (1, pl.ds(0, TOK))]
+    reads, writes = [], []
+    for n, (i, rows) in enumerate(cuts):
+        reads.append(pltpu.make_async_copy(ins[i].at[rows], held[i].at[rows], sems.at[0, n]))
+        writes.append(pltpu.make_async_copy(sources[i].at[rows], outs[i].at[rows], sems.at[1, n]))
     for read in reads:
         read.start()
-    for i in (0, 4, 3, 1, 2):
-        reads[i].wait()
+    for (i, _), read, write in zip(cuts, reads, writes):
+        read.wait()
         if i == 1:
             scaled[0][...] = held[1][...].astype(F32) / math.sqrt(KEPT * P_SIZE)
         if i == 2:
             scaled[1][...] = held[2][...].astype(F32) * math.sqrt(N / (KEPT * P_SIZE * D))
-        writes[i].start()
+        write.start()
     for write in writes:
         write.wait()
 
@@ -790,7 +801,7 @@
             buf((TOK, WIDE), BF), buf((GROUP, TOK), F32), buf((TOK, WIDE), BF),
             *ring(TOK // 2, COLS), *ring(TOK // 2, COLS), *ring(COLS, TOK),
             dma((5,)), dma((2,)), dma((2, 2, 2)), dma((2, 2, 4)), dma((2, 2, 4)), dma((2, 2, 2, 4)), dma((2, 2, 4)),
-            dma((2, 4)), dma((2, 2, 6)), dma((2, 6)), dma((2, N_CTX)), dma((4, N_CTX)), dma((4, N_CTX)),
+            dma((2, 2, 4)), dma((2, 2, 6)), dma((2, 6)), dma((2, N_CTX)), dma((4, N_CTX)), dma((4, N_CTX)),
             dma((4, N_HEAD)), dma((4, N_HEAD)), dma((5,)),
         ],
         compiler_params=pltpu.CompilerParams(
@@ -805,7 +816,7 @@
         out_shape=outs,
         in_specs=[hbm] * 5,
         out_specs=[hbm] * 5,
-        scratch_shapes=[*(buf(out.shape, out.dtype) for out in (*held, *outs[1:3])), dma((2, 5))],
+        scratch_shapes=[*(buf(out.shape, out.dtype) for out in (*held, *outs[1:3])), dma((2, 11))],
         compiler_params=pltpu.CompilerParams(has_side_effects=True, vmem_limit_bytes=VMEM_LIMIT),
     )(*results)
 

time: 112 us -> 110 us (0.982)
  Pallas kernels: 111 us -> 109 us
    pallas_call x1, Pallas kernels: 108 us -> 107 us  [per_device(): pl.pallas_call(kernel, out_shape=held, in_specs=[pl.BlockSpec(memory_spac...]
where the time goes in v5:
time: 110 us
  Pallas kernels  109 us (99%)
    pallas_call x1, Pallas kernels, per_device(): pl.pallas_call(kernel, out_shape=held, in_specs=[pl.BlockSpec(memory_spac...  107 us
    pallas_call x1, Pallas kernels, per_device(): pl.pallas_call(hand_over, out_shape=outs, in_specs=[hbm] * 5, out_specs=[...  2.63 us

profile of v5, /device:TPU:1, one launch (start us, length us, event | category | flops | bytes accessed | tf_op | source)
XLA Modules:
  0.0 110.1 jit_solution(13564487536611961584)
XLA Ops:
  0.6 106.6 %shard_map.110 = (bf16[512,1024]{1,0:T(8,128)(2,1)}, bf16[512,128]{1,0:T(8,128)(2,1)}, bf16[512,128]{1,0:T(8,128)(2,1)}, f32[16,512]{1,0:T(8,128)}, bf16[512,1024]{1,0:T(8,128)(2,1)}) custom-call(s32[64]{0:T(128)} %kept.1, bf16[2,2,128,1024]{3,2,1,0:T(8,128)(2,1)} %bitcast.1, bf16[512,1024]{1,0:T(8,128)(2,1)} %w_in.1, bf16[512,1024]{1,0:T(8,128)(2,1)} %x_in.1, ...), custom_call_target="tpu_custom_call" | custom-call | flops 14000000000 | bytes 8000000 | tf_op jit(solution)/shard_map/pallas_call | solution.py:782
  107.2 2.6 %shard_map.111 = (bf16[512,1024]{1,0:T(8,128)(2,1)}, f32[512,128]{1,0:T(8,128)}, f32[512,128]{1,0:T(8,128)}, f32[16,512]{1,0:T(8,128)}, bf16[512,1024]{1,0:T(8,128)(2,1)}) custom-call(bf16[512,1024]{1,0:T(8,128)(2,1)} %get-tuple-element.10.refs_0_, bf16[512,128]{1,0:T(8,128)(2,1)} %get-tuple-element.11.refs_1_, bf16[512,128]{1,0:T(8,128)(2,1)} %get-tuple-element.12.refs_2_, ...), custom_call_target="tpu_custom_call" | custom-call | tf_op jit(solution)/shard_map/pallas_call | solution.py:814

commit v6 on v5

--- a/solution.py
+++ b/solution.py
@@ -592,8 +592,8 @@
         B0[rows, :] = dot(sg, c[rows, :], TN)
         CP[rows, :] = (dot(sg, b[rows, :]) + dot(GH[rows, :], STIN[s].astype(BF), NT)).astype(BF)
 
+    x_rest(1)
     x_forward(0)
-    x_rest(1)
     w_gathers[0].forward()
     y_gathers[0].forward()
     w_gathers[1].forward()

time: 110 us -> 109 us (level)
  no operation moved by 1% of the time
where the time goes in v6:
time: 109 us
  Pallas kernels  108 us (99%)
    pallas_call x1, Pallas kernels, per_device(): pl.pallas_call(kernel, out_shape=held, in_specs=[pl.BlockSpec(memory_spac...  106 us
    pallas_call x1, Pallas kernels, per_device(): pl.pallas_call(hand_over, out_shape=outs, in_specs=[hbm] * 5, out_specs=[...  2.63 us

profile of v6, /device:TPU:1, one launch (start us, length us, event | category | flops | bytes accessed | tf_op | source)
XLA Modules:
  0.0 109.0 jit_solution(18056469410063737474)
XLA Ops:
  0.6 105.5 %shard_map.110 = (bf16[512,1024]{1,0:T(8,128)(2,1)}, bf16[512,128]{1,0:T(8,128)(2,1)}, bf16[512,128]{1,0:T(8,128)(2,1)}, f32[16,512]{1,0:T(8,128)}, bf16[512,1024]{1,0:T(8,128)(2,1)}) custom-call(s32[64]{0:T(128)} %kept.1, bf16[2,2,128,1024]{3,2,1,0:T(8,128)(2,1)} %bitcast.1, bf16[512,1024]{1,0:T(8,128)(2,1)} %w_in.1, bf16[512,1024]{1,0:T(8,128)(2,1)} %x_in.1, ...), custom_call_target="tpu_custom_call" | custom-call | flops 14000000000 | bytes 8000000 | tf_op jit(solution)/shard_map/pallas_call | solution.py:782
  106.1 2.6 %shard_map.111 = (bf16[512,1024]{1,0:T(8,128)(2,1)}, f32[512,128]{1,0:T(8,128)}, f32[512,128]{1,0:T(8,128)}, f32[16,512]{1,0:T(8,128)}, bf16[512,1024]{1,0:T(8,128)(2,1)}) custom-call(bf16[512,1024]{1,0:T(8,128)(2,1)} %get-tuple-element.10.refs_0_, bf16[512,128]{1,0:T(8,128)(2,1)} %get-tuple-element.11.refs_1_, bf16[512,128]{1,0:T(8,128)(2,1)} %get-tuple-element.12.refs_2_, ...), custom_call_target="tpu_custom_call" | custom-call | tf_op jit(solution)/shard_map/pallas_call | solution.py:814
